TPU v7x, 256 devices: a whole 4x4x8 slice. The times are simulated.
256 devices in a mesh: panel: 2 (over z_lo), tile: 32 (over z_hi, y, core), rad: 4 (over x).
Axes of the slice: x: 4, y: 4, z: 8 (z_hi: 4, z_lo: 2; z = z_hi * 2 + z_lo), core: 2. Of those that a mesh axis runs over, the one named last changes fastest.
Arguments:
- state: float32 [2, 8, 32, 1024, 512], P('panel', None, 'rad', 'tile'), may hold values from -2.5 to 2.5
- donor_base: int32 [2, 32, 32, 4], P('panel', 'tile'), may hold values from 0 to 15870, as said below
- fractions: float32 [2, 32, 2, 32, 4], P('panel', 'tile'), may hold values from 0 to 1
- dest_pos: int32 [2, 32, 32, 4], P('panel', 'tile'), may hold values from 0 to 127, as said below
Outputs:
- new_state: float32 [2, 8, 32, 1024, 512], P('panel', None, 'rad', 'tile')
Inputs may be any that keep to these rules, and one draw needn't show every extreme that they name: `donor_base`: each entry is phi * 512 + theta with phi below 31 and theta below 511, so that all four stencil cells lie in the donor tile. `dest_pos`: for each panel and tile, the 32 x 4 entries name every border point 0 to 127 exactly once.
All inputs are finite; a program needn't handle non-finite values.
Results may differ from a plain program's by a relative error of at most 0.00005.
Values sent between devices are 32-bit elements; how exact they have to be, the bound alone decides.
No kernel may reach another device: no remote copies, remote signals or barrier semaphores. Data moves between devices by JAX's collectives and lax.ppermute only.
A program may use at most 128 MiB of HBM per device.

v0:
```python
import math

import jax
import jax.numpy as jnp
from jax import lax
from jax.sharding import PartitionSpec as P

BASE_RADIUS = 0.6
EXACT = lax.Precision.HIGHEST


def swapped(block, axis, apart):
    count = lax.axis_size(axis)
    route = []
    for low in range(count):
        high = low | 1 << apart
        if high != low and high < count:
            route += [(low, high), (high, low)]
    return lax.ppermute(block, axis, route)


def extended(x, sides, width):
    for axis, dim in sides:
        peers, length = (lax.axis_size(axis), x.shape[dim])
        up = [(i, (i + 1) % peers) for i in range(peers - 1)]
        down = [(j, i) for i, j in up]
        last = lax.slice_in_dim(x, length - width, length, axis=dim)
        first = lax.slice_in_dim(x, 0, width, axis=dim)
        before = lax.ppermute(last, axis, up)
        after = lax.ppermute(first, axis, down)
        x = jnp.concatenate([before, x, after], axis=dim)
    return x


def geometry(theta_count, phi_count):
    theta_step = 0.5 * math.pi / theta_count
    phi_step = 1.5 * math.pi / phi_count
    shell_step = 0.6 * min(theta_step, phi_step)
    corner = BASE_RADIUS * math.sin(0.25 * math.pi)
    spacing = min(shell_step, corner * theta_step, corner * phi_step)
    return (theta_step, phi_step, shell_step, spacing)


def first_four(padded, axis, length):

    def piece(offset):
        return lax.slice_in_dim(padded, offset, offset + length, axis=axis)

    return (piece(0) - 8.0 * piece(1) + 8.0 * piece(3) - piece(4)) / 12.0


def second_four(padded, axis, length):

    def piece(offset):
        return lax.slice_in_dim(padded, offset, offset + length, axis=axis)

    return (-piece(0) + 16.0 * piece(1) - 30.0 * piece(2) + 16.0 * piece(3) - piece(4)) / 12.0


def theta_pieces(center):
    rows = center.shape[3]
    position = jnp.arange(rows, dtype=jnp.int32)
    pieces = []
    for offset in range(5):
        delta = offset - 2
        if delta == 0:
            pieces.append(center)
        else:
            inside = ((position + delta >= 0) & (position + delta < rows)).reshape(1, 1, 1, rows)
            rolled = jnp.roll(center, -delta, axis=3)
            pieces.append(jnp.where(inside, rolled, 0.0))
    return pieces


def section_update(
    center, phi_padded, shell_padded, radius, colat, theta_step, phi_step, shell_step, spacing
):
    shells = center.shape[1]
    cols = center.shape[2]
    rows = center.shape[3]
    pieces = theta_pieces(center)
    theta_first = (pieces[0] - 8.0 * pieces[1] + 8.0 * pieces[3] - pieces[4]) / 12.0
    theta_second = (
        -pieces[0] + 16.0 * pieces[1] - 30.0 * pieces[2] + 16.0 * pieces[3] - pieces[4]
    ) / 12.0
    inner = lax.slice_in_dim(shell_padded, 0, shells, axis=1)
    outer = lax.slice_in_dim(shell_padded, 2, shells + 2, axis=1)
    grad_shell = (outer - inner) * (0.5 / shell_step)
    lap_shell = (outer - 2.0 * center + inner) * (1.0 / (shell_step * shell_step))
    theta_scale = (1.0 / (radius * theta_step)).reshape(1, shells, 1, 1)
    phi_scale = (1.0 / (radius[:, None] * jnp.sin(colat)[None, :] * phi_step)).reshape(
        1, shells, 1, rows
    )
    grad_theta = theta_first * theta_scale
    grad_phi = first_four(phi_padded, 2, cols) * phi_scale
    laplace = lap_shell + theta_second * (theta_scale * theta_scale)
    laplace = laplace + second_four(phi_padded, 2, cols) * (phi_scale * phi_scale)
    lnrho = center[0]
    velocity = center[1:4]
    magnetic = center[4:7]
    pressure = center[7]
    advect = velocity[0] * grad_shell + velocity[1] * grad_theta + velocity[2] * grad_phi
    along_field = magnetic[0] * grad_shell + magnetic[1] * grad_theta + magnetic[2] * grad_phi
    diverge = grad_shell[1] + grad_theta[2] + grad_phi[3]
    inv_rho = jnp.exp(-lnrho)
    grad_press = jnp.stack([grad_shell[7], grad_theta[7], grad_phi[7]])
    rate_rho = -advect[0] - diverge
    rate_vel = (
        -advect[1:4]
        - inv_rho * grad_press
        + inv_rho * along_field[4:7]
        + 0.25 * spacing * laplace[1:4]
    )
    rate_mag = -advect[4:7] + along_field[1:4] - magnetic * diverge + 0.2 * spacing * laplace[4:7]
    rate_press = -advect[7] - 5.0 / 3.0 * pressure * diverge + 0.3 * spacing * laplace[7]
    rates = jnp.concatenate([rate_rho[None], rate_vel, rate_mag, rate_press[None]], axis=0)
    return center + 0.2 * spacing * rates


def deliver(payload):
    moved = lax.all_to_all(payload, "tile", split_axis=0, concat_axis=0, tiled=True)
    return swapped(moved, "panel", 0)


def on_device(state, donor_base, fractions, dest_pos):
    fields = state[0]
    count, shells, cols, rows = fields.shape
    tiles = lax.axis_size("tile")
    stacked = count * shells
    cells = cols * rows
    flat = fields.reshape(stacked, cells)
    base = donor_base[0, 0].reshape(-1)
    frac_theta = fractions[0, 0, 0].reshape(-1)
    frac_phi = fractions[0, 0, 1].reshape(-1)
    weights = (
        (1.0 - frac_phi) * (1.0 - frac_theta),
        (1.0 - frac_phi) * frac_theta,
        frac_phi * (1.0 - frac_theta),
        frac_phi * frac_theta,
    )
    offsets = (0, 1, rows, rows + 1)
    grid = jnp.arange(cells, dtype=jnp.int32)[None, :]
    stencil = jnp.zeros((base.shape[0], cells), jnp.float32)
    for offset, weight in zip(offsets, weights):
        stencil = stencil + jnp.where(grid == (base + offset)[:, None], weight[:, None], 0.0)
    payload = jnp.einsum("ng,sg->ns", stencil, flat, precision=EXACT)
    payload = payload.reshape(tiles, -1, stacked)
    values = deliver(payload).reshape(-1, stacked)
    points = dest_pos[0, 0].reshape(-1)
    border_count = points.shape[0]
    placing = (jnp.arange(border_count, dtype=jnp.int32)[:, None] == points[None, :]).astype(
        jnp.float32
    )
    border = jnp.dot(placing, values, precision=EXACT).reshape(4, cols, stacked)
    edge_rows = jnp.array([0, 1, rows - 2, rows - 1], dtype=jnp.int32)
    row_index = jnp.arange(rows, dtype=jnp.int32)
    selector = (row_index[None, :] == edge_rows[:, None]).astype(jnp.float32)
    spread = jnp.einsum("qcs,qr->scr", border, selector, precision=EXACT).reshape(
        count, shells, cols, rows
    )
    edge_mask = ((row_index < 2) | (row_index >= rows - 2)).reshape(1, 1, 1, rows)
    fields = jnp.where(edge_mask, spread, fields)
    phi_padded = extended(fields, (("tile", 2),), 2)
    shell_padded = extended(fields, (("rad", 1),), 1)
    theta_step, phi_step, shell_step, spacing = geometry(rows, cols * tiles)
    colat = (
        0.25 * math.pi + (jnp.arange(rows, dtype=jnp.int32).astype(jnp.float32) + 0.5) * theta_step
    )
    layer = lax.axis_index("rad") * shells + jnp.arange(shells, dtype=jnp.int32)
    radius = BASE_RADIUS + (layer.astype(jnp.float32) + 0.5) * shell_step
    updated = section_update(
        fields, phi_padded, shell_padded, radius, colat, theta_step, phi_step, shell_step, spacing
    )
    return updated[None]


def solution(mesh):
    placed = (
        P("panel", None, "rad", "tile", None),
        P("panel", "tile", None, None),
        P("panel", "tile", None, None, None),
        P("panel", "tile", None, None),
    )
    return jax.shard_map(
        on_device,
        mesh=mesh,
        in_specs=placed,
        out_specs=P("panel", None, "rad", "tile", None),
        check_vma=False,
    )
```

profile of v0, /device:TPU:4, one launch (start us, length us, event | category | flops | bytes accessed | tf_op | source)
XLA Modules:
  0.0 137.1 jit_solution(2252402150314134343)
XLA Ops:
  0.0 0.7 broadcast_add_fusion.2
  0.7 0.7 fusion.62
  1.4 4.9 %reshape.394 = f32[64,16384,1]{1,0,2:T(8,128)} reshape(f32[1,8,8,32,512]{4,3,2,1,0:T(8,128)} %param.5) | data formatting | bytes 8388608 | tf_op jit(solution)/shard_map/reshape;squeeze | solution.py:131
  6.3 13.1 %fusion = f32[32,4,64]{2,0,1:T(8,128)S(1)} fusion(f32[64,16384,1]{1,0,2:T(8,128)} %reshape.394, f32[32,4]{0,1:T(4,128)S(1)} %get-tuple-element.40, s32[32,4]{0,1:T(4,128)S(1)} %get-tuple-element.45, f32[32,4]{0,1:T(4,128)S(1)} %get-tuple-element.39, s32[32,4]{0,1:T(4,128)S(1)} %get-tuple-element.44, f32[32,4]{0,1:T(4,128)S(1)} %get-tuple-element.38, ...), kind=kOutput, calls=%fused_computation | convolution fusion | flops 1633681408 | bytes 4231168 | tf_op jit(solution)/shard_map/ng,sg->ns/dot_general | solution.py:146
  19.5 0.7 reshape.398
  20.2 11.5 %all-to-all-start = ((f32[32,1,256]{2,1,0:T(1,128)}), f32[32,1,256]{2,1,0:T(1,128)S(1)}, u32[]{:S(2)}, u32[]{:S(2)}) async-start(f32[32,1,256]{2,1,0:T(1,128)} %reshape.398), calls=%async_computation | async-start | bytes 65536 | tf_op jit(solution)/shard_map/all_to_all | solution.py:121
  31.7 0.6 multiply_multiply_fusion.1
  32.4 0.5 fusion.59
  32.9 0.7 fusion.45
  33.6 0.6 fusion.57
  34.2 7.4 %all-to-all-done = f32[32,1,256]{2,1,0:T(1,128)S(1)} async-done(((f32[32,1,256]{2,1,0:T(1,128)}), f32[32,1,256]{2,1,0:T(1,128)S(1)}, u32[]{:S(2)}, u32[]{:S(2)}) %all-to-all-start) | async-done | bytes 32800 | tf_op jit(solution)/shard_map/all_to_all | solution.py:121
  41.6 0.5 broadcast.558
  42.1 0.7 reduce
  42.8 0.1 reshape.399
  42.9 1.1 collective-permute-start
  44.0 0.1 copy.13
  44.1 0.1 eq.156
  44.2 0.0 copy-start
  44.2 3.1 %collective-permute-done = f32[32,4,64]{2,1,0:T(4,128)S(1)} collective-permute-done((f32[32,4,64]{2,1,0:T(4,128)S(1)}, f32[32,4,64]{2,1,0:T(4,128)S(1)}, u32[]{:S(2)}, u32[]{:S(2)}) %collective-permute-start) | collective-permute-done | bytes 32800 | tf_op jit(solution)/shard_map/ppermute | solution.py:19
  47.3 0.2 fusion.41
  47.5 1.9 %fusion.39 = f32[512,32,64]{0,2,1:T(8,128)S(1)} fusion(f32[4,32,64]{2,1,0:T(8,128)S(1)} %fusion.41, s32[4]{0:T(128)S(1)} %copy-done.13), kind=kOutput, calls=%fused_computation.85 | convolution fusion | flops 50333696 | bytes 4227088 | tf_op jit(solution)/shard_map/qcs,qr->scr/dot_general | solution.py:158
  49.4 3.0 %bitcast_select_fusion = f32[8,8,32,512]{3,2,1,0:T(8,128)S(1)} fusion(f32[1,8,8,32,512]{4,3,2,1,0:T(8,128)S(1)} %copy-done, f32[8,8,32,512]{3,1,0,2:T(8,128)S(1)} %bitcast.65, pred[512]{0:T(512)(128)(4,1)S(1)} %fusion.61), kind=kLoop, calls=%fused_computation.29 | loop fusion | flops 1048576 | bytes 12583424 | tf_op jit(solution)/shard_map/jit(_where)/select_n | solution.py:162
  52.4 0.2 fusion.69
  52.7 0.1 fusion.68
  52.8 1.7 %fusion.38 = (f32[8,32,512]{2,1,0:T(8,128)}, f32[8,32,512]{2,1,0:T(8,128)}, f32[8,32,512]{2,1,0:T(8,128)}, f32[8,32,512]{2,1,0:T(8,128)}, f32[8,32,512]{2,1,0:T(8,128)}, /*index=5*/f32[8,32,512]{2,1,0:T(8,128)}) fusion(f32[8,8,32,512]{3,2,1,0:T(8,128)S(1)} %bitcast_select_fusion), kind=kLoop, calls=%fused_computation.84 | loop fusion | flops 262144 | bytes 6291456 | tf_op jit(solution)/shard_map/mul | solution.py:102
  54.5 3.8 %fusion.67 = (f32[8,8,32,511]{3,2,1,0:T(8,128)S(1)}, f32[8,8,32,511]{3,2,1,0:T(8,128)}) fusion(f32[8,8,32,512]{3,2,1,0:T(8,128)S(1)} %bitcast_select_fusion), kind=kLoop, calls=%fused_computation.135 | loop fusion | bytes 16744448 | tf_op jit(solution)/shard_map/jit(_roll_static)/slice | solution.py:70
  58.3 4.9 %fusion.65 = (f32[8,8,32,510]{3,2,1,0:T(8,128)}, f32[8,8,32,510]{3,2,1,0:T(8,128)}) fusion(f32[8,8,32,512]{3,2,1,0:T(8,128)S(1)} %bitcast_select_fusion), kind=kLoop, calls=%fused_computation.133 | loop fusion | bytes 16711680 | tf_op jit(solution)/shard_map/jit(_roll_static)/slice | solution.py:70
  63.1 1.5 %collective-permute-start.4 = (f32[8,8,2,512]{3,2,1,0:T(2,128)S(1)}, f32[8,8,2,512]{3,2,1,0:T(2,128)S(1)}, u32[]{:S(2)}, u32[]{:S(2)}) collective-permute-start(f32[8,8,2,512]{3,2,1,0:T(2,128)S(1)} %get-tuple-element.35), channel_id=1, source_target_pairs={{4,0},{8,4},{12,8},{16,12},{20,16},{24,20},{28,24},{32,28},{36,32}... | collective-permute-start | bytes 786440 | tf_op jit(solution)/shard_map/ppermute | solution.py:30
  64.6 3.0 %collective-permute-start.3 = (f32[8,8,2,512]{3,2,1,0:T(2,128)S(1)}, f32[8,8,2,512]{3,2,1,0:T(2,128)S(1)}, u32[]{:S(2)}, u32[]{:S(2)}) collective-permute-start(f32[8,8,2,512]{3,2,1,0:T(2,128)S(1)} %get-tuple-element.36), channel_id=1, source_target_pairs={{0,4},{4,8},{8,12},{12,16},{16,20},{20,24},{24,28},{28,32},{32,36}... | collective-permute-start | bytes 786440 | tf_op jit(solution)/shard_map/ppermute | solution.py:29
  67.7 3.1 %collective-permute-start.2 = (f32[8,1,32,512]{3,2,1,0:T(8,128)S(1)}, f32[8,1,32,512]{3,2,1,0:T(8,128)S(1)}, u32[]{:S(2)}, u32[]{:S(2)}) collective-permute-start(f32[8,1,32,512]{3,2,1,0:T(8,128)S(1)} %get-tuple-element.33), channel_id=1, source_target_pairs={{0,1},{1,2},{2,3},{4,5},{5,6},{6,7},{8,9},{9,10},{10,11},{12,13},{... | collective-permute-start | bytes 1572872 | tf_op jit(solution)/shard_map/ppermute | solution.py:29
  70.8 2.7 %collective-permute-start.1 = (f32[8,1,32,512]{3,2,1,0:T(8,128)S(1)}, f32[8,1,32,512]{3,2,1,0:T(8,128)}, u32[]{:S(2)}, u32[]{:S(2)}) collective-permute-start(f32[8,1,32,512]{3,2,1,0:T(8,128)S(1)} %get-tuple-element.34), channel_id=1, source_target_pairs={{1,0},{2,1},{3,2},{5,4},{6,5},{7,6},{9,8},{10,9},{11,10},{13,12},{... | collective-permute-start | bytes 1572872 | tf_op jit(solution)/shard_map/ppermute | solution.py:30
  73.5 0.4 fusion.66
  73.9 1.7 %fusion.64 = (f32[8,8,32,2]{3,2,1,0:T(8,128)}, f32[8,8,32,2]{3,2,1,0:T(8,128)}) fusion(f32[8,8,32,512]{3,2,1,0:T(8,128)S(1)} %bitcast_select_fusion), kind=kLoop, calls=%fused_computation.132 | loop fusion | bytes 65536 | tf_op jit(solution)/shard_map/jit(_roll_static)/slice | solution.py:70
  75.6 0.0 collective-permute-done.4
  75.6 0.0 collective-permute-done.3
  75.7 7.9 %collective-permute-done.2 = f32[8,1,32,512]{3,2,1,0:T(8,128)S(1)} collective-permute-done((f32[8,1,32,512]{3,2,1,0:T(8,128)S(1)}, f32[8,1,32,512]{3,2,1,0:T(8,128)S(1)}, u32[]{:S(2)}, u32[]{:S(2)}) %collective-permute-start.2) | collective-permute-done | bytes 524320 | tf_op jit(solution)/shard_map/ppermute | solution.py:29
  83.6 2.9 %collective-permute-done.1 = f32[8,1,32,512]{3,2,1,0:T(8,128)} collective-permute-done((f32[8,1,32,512]{3,2,1,0:T(8,128)S(1)}, f32[8,1,32,512]{3,2,1,0:T(8,128)}, u32[]{:S(2)}, u32[]{:S(2)}) %collective-permute-start.1) | collective-permute-done | bytes 524320 | tf_op jit(solution)/shard_map/ppermute | solution.py:30
  86.5 0.0 copy-done.6
  86.5 15.0 %multiply_add_fusion.1 = (f32[8,8,32,512]{3,2,1,0:T(8,128)}, f32[8,8,32,512]{3,2,1,0:T(8,128)}, f32[8,8,32,512]{3,2,1,0:T(8,128)}) fusion(f32[8,32,512]{2,1,0:T(8,128)} %get-tuple-element.20, f32[8,32,512]{2,1,0:T(8,128)} %get-tuple-element.21, f32[8,32,512]{2,1,0:T(8,128)} %get-tuple-element.22, f32[8,8,32,512]{3,2,1,0:T(8,128)S(1)} %bitcast_select_fusion, ...), kind=kLoop, calls=%fused_computation.32 | loop fusion | flops 33554432 | bytes 36718624 | tf_op jit(solution)/shard_map/add | solution.py:103
  101.5 7.1 %broadcast_multiply_fusion = (f32[8,8,32,512]{3,2,1,0:T(8,128)}, f32[8,8,32,512]{3,2,1,0:T(8,128)}) fusion(f32[8,8,32,512]{3,2,1,0:T(8,128)S(1)} %bitcast_select_fusion, f32[8,1,32,512]{3,2,1,0:T(8,128)S(1)} %collective-permute-done.2, f32[8,1,32,512]{3,2,1,0:T(8,128)} %collective-permute-done.1, f32[8,8,32,512]{3,2,1,0:T(8,128)} %get-tuple-element.9, ...), kind=kLoop, calls=%fused_computation.46 | loop fusion | flops 9437184 | bytes 23592960 | tf_op jit(solution)/shard_map/mul | solution.py:88
  108.6 0.0 copy-start.3
  108.7 3.8 %fusion.37 = (f32[1,1,8,32,512]{4,3,2,1,0:T(8,128)}, f32[1,8,32,512]{3,2,1,0:T(8,128)}, f32[1,8,32,512]{3,2,1,0:T(8,128)}, f32[1,8,32,512]{3,2,1,0:T(8,128)}, f32[1,8,32,512]{3,2,1,0:T(8,128)}) fusion(f32[8,8,32,512]{3,2,1,0:T(8,128)} %get-tuple-element.13, f32[8,8,32,512]{3,2,1,0:T(8,128)} %get-tuple-element.9, f32[8,8,32,512]{3,2,1,0:T(8,128)} %get-tuple-element.8, ...), kind=kLoop, calls=%fused_computation.80 | loop fusion | flops 524288 | bytes 6291456 | tf_op jit(solution)/shard_map/concatenate | solution.py:116
  112.5 0.2 copy-done.2
  112.7 0.7 copy-done.3
  113.5 10.7 %multiply_add_fusion = f32[8,8,32,512]{3,2,1,0:T(8,128)} fusion(f32[8,8,32,512]{3,2,1,0:T(8,128)S(1)} %bitcast_select_fusion, f32[8,8,2,512]{3,2,1,0:T(2,128)} %copy-done.6, f32[8,8,2,512]{3,2,1,0:T(2,128)} %copy-done.5, f32[8,1,32,512]{3,2,1,0:T(8,128)} %collective-permute-done.1, f32[8,1,32,512]{3,2,1,0:T(8,128)S(1)} %collective-permute-done.2, ...), kind=kLoop, calls=%fused_computation.31 | loop fusion | flops 38797312 | bytes 26757152 | tf_op jit(solution)/shard_map/add | solution.py:97
  124.2 1.7 %fusion.35 = (f32[8,32,512]{2,1,0:T(8,128)S(1)}, f32[1,1,8,32,512]{4,3,2,1,0:T(8,128)S(1)}) fusion(f32[8,8,32,512]{3,2,1,0:T(8,128)S(1)} %bitcast_select_fusion, f32[8,8,32,512]{3,2,1,0:T(8,128)} %multiply_add_fusion, f32[1,8,32,512]{3,2,1,0:T(8,128)} %get-tuple-element.6, f32[8,8,32,512]{3,2,1,0:T(8,128)} %get-tuple-element.13), kind=kLoop, calls=%fused_computation.75 | loop fusion | flops 917504 | bytes 3670016 | tf_op jit(solution)/shard_map/mul | solution.py:110
  125.9 6.0 %fusion.26 = (f32[1,3,8,32,512]{4,3,2,1,0:T(8,128)S(1)}, f32[1,3,8,32,512]{4,3,2,1,0:T(8,128)S(1)}) fusion(f32[8,8,32,512]{3,2,1,0:T(8,128)} %multiply_add_fusion, f32[8,8,32,512]{3,2,1,0:T(8,128)} %get-tuple-element.7, f32[8,8,32,512]{3,2,1,0:T(8,128)} %get-tuple-element.13, f32[1,8,32,512]{3,2,1,0:T(8,128)} %get-tuple-element.18, ...), kind=kLoop, calls=%fused_computation.56 | loop fusion | flops 5898240 | bytes 16777216 | tf_op jit(solution)/shard_map/concatenate | solution.py:116
  131.9 5.2 %fusion.11 = f32[1,8,8,32,512]{4,3,2,1,0:T(8,128)} fusion(f32[1,1,8,32,512]{4,3,2,1,0:T(8,128)S(1)} %get-tuple-element.15, f32[1,3,8,32,512]{4,3,2,1,0:T(8,128)S(1)} %get-tuple-element.11, f32[1,3,8,32,512]{4,3,2,1,0:T(8,128)S(1)} %get-tuple-element.10, f32[1,1,8,32,512]{4,3,2,1,0:T(8,128)S(1)} %copy-done.4, f32[1,8,8,32,512]{4,3,2,1,0:T(8,128)S(1)} %copy-done, ...), kind=kLoop, calls=%fused_computation.28 | loop fusion | flops 6291456 | bytes 16777728 | tf_op jit(solution)/shard_map/add | solution.py:117
  (30 shorter events, 0.2 us)
Async XLA Ops:
  1.4 5.0 %copy-start.9 = (s32[1,1,32,4]{2,3,1,0:T(4,128)S(1)}, s32[1,1,32,4]{2,3,1,0:T(4,128)}, u32[]{:S(2)}) copy-start(s32[1,1,32,4]{2,3,1,0:T(4,128)} %param.6) | copy-start | bytes 1540
  6.3 37.7 %copy-start.8 = (s32[1,1,32,4]{2,3,1,0:T(4,128)S(1)}, s32[1,1,32,4]{2,3,1,0:T(4,128)}, u32[]{:S(2)}) copy-start(s32[1,1,32,4]{2,3,1,0:T(4,128)} %param.8) | copy-start | bytes 1540
  6.3 41.2 %copy-start.13 = (s32[4]{0:T(128)S(1)}, s32[4]{0:T(128)}, u32[]{:S(2)}) copy-start(s32[4]{0:T(128)} %constant.30.clone) | copy-start | bytes 52
  20.2 21.3 %all-to-all-start = ((f32[32,1,256]{2,1,0:T(1,128)}), f32[32,1,256]{2,1,0:T(1,128)S(1)}, u32[]{:S(2)}, u32[]{:S(2)}) async-start(f32[32,1,256]{2,1,0:T(1,128)} %reshape.398), calls=%async_computation | async-start | bytes 65536 | tf_op jit(solution)/shard_map/all_to_all | solution.py:121
  42.9 4.4 %collective-permute-start = (f32[32,4,64]{2,1,0:T(4,128)S(1)}, f32[32,4,64]{2,1,0:T(4,128)S(1)}, u32[]{:S(2)}, u32[]{:S(2)}) collective-permute-start(f32[32,4,64]{2,1,0:T(4,128)S(1)} %reshape.399), channel_id=1, source_target_pairs={{0,128},{128,0},{1,129},{129,1},{2,130},{130,2},{3,131},{131,3},{4... | collective-permute-start | bytes 98312 | tf_op jit(solution)/shard_map/ppermute | solution.py:19
  44.2 5.2 %copy-start = (f32[1,8,8,32,512]{4,3,2,1,0:T(8,128)S(1)}, f32[1,8,8,32,512]{4,3,2,1,0:T(8,128)}, u32[]{:S(2)}) copy-start(f32[1,8,8,32,512]{4,3,2,1,0:T(8,128)} %param.5) | copy-start | bytes 12582916
  63.1 12.5 %collective-permute-start.4 = (f32[8,8,2,512]{3,2,1,0:T(2,128)S(1)}, f32[8,8,2,512]{3,2,1,0:T(2,128)S(1)}, u32[]{:S(2)}, u32[]{:S(2)}) collective-permute-start(f32[8,8,2,512]{3,2,1,0:T(2,128)S(1)} %get-tuple-element.35), channel_id=1, source_target_pairs={{4,0},{8,4},{12,8},{16,12},{20,16},{24,20},{28,24},{32,28},{36,32}... | collective-permute-start | bytes 786440 | tf_op jit(solution)/shard_map/ppermute | solution.py:30
  64.6 11.0 %collective-permute-start.3 = (f32[8,8,2,512]{3,2,1,0:T(2,128)S(1)}, f32[8,8,2,512]{3,2,1,0:T(2,128)S(1)}, u32[]{:S(2)}, u32[]{:S(2)}) collective-permute-start(f32[8,8,2,512]{3,2,1,0:T(2,128)S(1)} %get-tuple-element.36), channel_id=1, source_target_pairs={{0,4},{4,8},{8,12},{12,16},{16,20},{20,24},{24,28},{28,32},{32,36}... | collective-permute-start | bytes 786440 | tf_op jit(solution)/shard_map/ppermute | solution.py:29
  67.7 15.9 %collective-permute-start.2 = (f32[8,1,32,512]{3,2,1,0:T(8,128)S(1)}, f32[8,1,32,512]{3,2,1,0:T(8,128)S(1)}, u32[]{:S(2)}, u32[]{:S(2)}) collective-permute-start(f32[8,1,32,512]{3,2,1,0:T(8,128)S(1)} %get-tuple-element.33), channel_id=1, source_target_pairs={{0,1},{1,2},{2,3},{4,5},{5,6},{6,7},{8,9},{9,10},{10,11},{12,13},{... | collective-permute-start | bytes 1572872 | tf_op jit(solution)/shard_map/ppermute | solution.py:29
  70.8 15.7 %collective-permute-start.1 = (f32[8,1,32,512]{3,2,1,0:T(8,128)S(1)}, f32[8,1,32,512]{3,2,1,0:T(8,128)}, u32[]{:S(2)}, u32[]{:S(2)}) collective-permute-start(f32[8,1,32,512]{3,2,1,0:T(8,128)S(1)} %get-tuple-element.34), channel_id=1, source_target_pairs={{1,0},{2,1},{3,2},{5,4},{6,5},{7,6},{9,8},{10,9},{11,10},{13,12},{... | collective-permute-start | bytes 1572872 | tf_op jit(solution)/shard_map/ppermute | solution.py:30
  75.6 7.9 %copy-start.5 = (f32[8,8,2,512]{3,2,1,0:T(2,128)}, f32[8,8,2,512]{3,2,1,0:T(2,128)S(1)}, u32[]{:S(2)}) copy-start(f32[8,8,2,512]{3,2,1,0:T(2,128)S(1)} %collective-permute-done.4) | copy-start | bytes 786436
  75.7 10.9 %copy-start.6 = (f32[8,8,2,512]{3,2,1,0:T(2,128)}, f32[8,8,2,512]{3,2,1,0:T(2,128)S(1)}, u32[]{:S(2)}) copy-start(f32[8,8,2,512]{3,2,1,0:T(2,128)S(1)} %collective-permute-done.3) | copy-start | bytes 786436
  101.5 11.0 %copy-start.7 = (f32[8,512]{1,0:T(8,128)S(1)}, f32[8,512]{1,0:T(8,128)}, u32[]{:S(2)}) copy-start(f32[8,512]{1,0:T(8,128)} %get-tuple-element.42) | copy-start | bytes 49156
  108.6 3.9 %copy-start.1 = (f32[8,8,32,511]{3,2,1,0:T(8,128)S(1)}, f32[8,8,32,511]{3,2,1,0:T(8,128)}, u32[]{:S(2)}) copy-start(f32[8,8,32,511]{3,2,1,0:T(8,128)} %get-tuple-element.32) | copy-start | bytes 12558340
  108.6 4.1 %copy-start.2 = (f32[8,8,32,2]{3,2,1,0:T(8,128)S(1)}, f32[8,8,32,2]{3,2,1,0:T(8,128)}, u32[]{:S(2)}) copy-start(f32[8,8,32,2]{3,2,1,0:T(8,128)} %get-tuple-element.25) | copy-start | bytes 49156
  108.6 4.8 %copy-start.3 = (f32[8,8,32,2]{3,2,1,0:T(8,128)S(1)}, f32[8,8,32,2]{3,2,1,0:T(8,128)}, u32[]{:S(2)}) copy-start(f32[8,8,32,2]{3,2,1,0:T(8,128)} %get-tuple-element.26) | copy-start | bytes 49156
  108.6 4.8 %copy-start.10 = (pred[512]{0:T(512)(128)(4,1)S(1)}, pred[512]{0:T(512)(128)(4,1)}, u32[]{:S(2)}) copy-start(pred[512]{0:T(512)(128)(4,1)} %get-tuple-element.51) | copy-start | bytes 1540
  108.7 4.8 %copy-start.11 = (pred[512]{0:T(512)(128)(4,1)S(1)}, pred[512]{0:T(512)(128)(4,1)}, u32[]{:S(2)}) copy-start(pred[512]{0:T(512)(128)(4,1)} %get-tuple-element.48) | copy-start | bytes 1540
  108.7 4.8 %copy-start.12 = (pred[512]{0:T(512)(128)(4,1)S(1)}, pred[512]{0:T(512)(128)(4,1)}, u32[]{:S(2)}) copy-start(pred[512]{0:T(512)(128)(4,1)} %get-tuple-element.49) | copy-start | bytes 1540
  108.7 4.8 %copy-start.14 = (f32[8]{0:T(128)S(1)}, f32[8]{0:T(128)}, u32[]{:S(2)}) copy-start(f32[8]{0:T(128)} %get-tuple-element.46) | copy-start | bytes 100
  125.9 6.0 %copy-start.4 = (f32[1,1,8,32,512]{4,3,2,1,0:T(8,128)S(1)}, f32[1,1,8,32,512]{4,3,2,1,0:T(8,128)}, u32[]{:S(2)}) copy-start(f32[1,1,8,32,512]{4,3,2,1,0:T(8,128)} %get-tuple-element.5) | copy-start | bytes 1572868
where the time goes:
time: 138 us; the launch traced here: 137 us
  other arithmetic  58.8 us (43%)
  starting transfers between devices  22.9 us (17%)
  waiting for transfers between devices  21.3 us (15%)
  local copies, waits for them, and re-layouts  18.6 us (13%)
  matrix products  15.2 us (11%)
    add x1, other arithmetic, section_update(): magnetic[0] * grad_shell + magnetic[1] * grad_theta + magnetic[2] * grad_phi  15 us
    dot_general x1, matrix products, on_device(): payload = jnp.einsum('ng,sg->ns', stencil, flat, precision=EXACT)  13.1 us
    all_to_all x1, starting transfers between devices, deliver(): lax.all_to_all(payload, 'tile', split_axis=0, concat_axis=0, tiled=True)  11.5 us
    slice x4, local copies, waits for them, and re-layouts, theta_pieces(): rolled = jnp.roll(center, -delta, axis=3)  10.7 us
    add x1, other arithmetic, section_update(): laplace + second_four(phi_padded, 2, cols) * (phi_scale * phi_scale)  10.7 us
    concatenate x2, other arithmetic, section_update(): jnp.concatenate([rate_rho[None], rate_vel, rate_mag, rate_press[None]], a...  9.87 us
    ppermute x2, waiting for transfers between devices, extended(): before = lax.ppermute(last, axis, up)  7.91 us
    all_to_all x1, waiting for transfers between devices, deliver(): lax.all_to_all(payload, 'tile', split_axis=0, concat_axis=0, tiled=True)  7.43 us
  transfers between devices with their start and end apart: 6, of which 4 were waited for; matrix products, arithmetic and copies ran while one was open for 3% of the time, Pallas kernels for 0%

commit v1 on v0

v1 whole, which is shorter than its diff:
```python
import functools
import math

import jax
import jax.numpy as jnp
import numpy as np
from jax import lax
from jax.experimental import pallas as pl
from jax.experimental.pallas import tpu as pltpu
from jax.sharding import PartitionSpec as P

BASE_RADIUS = 0.6
F32 = jnp.float32
BF16 = jnp.bfloat16
LANES = 128
FIRST = 8
ROWS = 48


def geometry(theta_count, phi_count):
    theta_step = 0.5 * math.pi / theta_count
    phi_step = 1.5 * math.pi / phi_count
    shell_step = 0.6 * min(theta_step, phi_step)
    corner = BASE_RADIUS * math.sin(0.25 * math.pi)
    spacing = min(shell_step, corner * theta_step, corner * phi_step)
    return (theta_step, phi_step, shell_step, spacing)


def halves(x):
    high = x.astype(BF16)
    return high, (x - high.astype(F32)).astype(BF16)


def lane_order(table):
    tiles = table.shape[0]
    lane = lax.broadcasted_iota(jnp.int32, (tiles, LANES), 1)
    row = lax.broadcasted_iota(jnp.int32, (tiles, LANES), 0)
    slot = 2 * (lane // 64) + lane % 2
    wide = jnp.zeros((tiles, LANES), F32)
    for s in range(4):
        wide = jnp.where(slot == s, table[:, s : s + 1], wide)
    wide = jnp.where((lane % 64) // 2 == row, wide, 0.0)
    return jnp.sum(wide, axis=0, keepdims=True)


def payload_kernel(
    panel_ref, x_ref, base_ref, frac_ref, pay_ref, cols_ref, held, values, load_sem, cols_sem
):
    stacked, cols, rows = held.shape
    chunk = 8
    chunks = stacked // chunk

    def load(i):
        part = pl.ds(i * chunk, chunk)
        return pltpu.make_async_copy(x_ref.at[part], held.at[part], load_sem.at[i])

    def column(k, c):
        return pltpu.make_async_copy(x_ref.at[:, c, :], cols_ref.at[k], cols_sem.at[k])

    edges = ((0, 0), (1, 1), (2, cols - 2), (3, cols - 1))
    for i in range(chunks):
        load(i).start()
    for k, c in edges:
        column(k, c).start()
    base = lane_order(base_ref[...].astype(F32)).astype(jnp.int32)
    frac_theta = lane_order(frac_ref[0])
    frac_phi = lane_order(frac_ref[1])
    phi = base // rows
    theta = base - phi * rows
    position = lax.broadcasted_iota(jnp.int32, (rows, LANES), 0)
    along_theta = jnp.where(position == theta, 1.0 - frac_theta, 0.0)
    along_theta = along_theta + jnp.where(position == theta + 1, frac_theta, 0.0)
    high, low = halves(along_theta)
    both = jnp.concatenate([high, low], axis=1)
    place = lax.broadcasted_iota(jnp.int32, (cols, LANES), 0)
    along_phi = jnp.where(place == phi, 1.0 - frac_phi, 0.0)
    along_phi = along_phi + jnp.where(place == phi + 1, frac_phi, 0.0)
    for i in range(chunks):
        load(i).wait()
        x_high, x_low = halves(held[i * chunk : (i + 1) * chunk].reshape(chunk * cols, rows))
        wide = jnp.dot(x_high, both, preferred_element_type=F32)
        line = wide[:, :LANES] + wide[:, LANES:] + jnp.dot(x_low, high, preferred_element_type=F32)
        line = line.reshape(chunk, cols, LANES) * along_phi[None]
        values[i * chunk : (i + 1) * chunk, :] = jnp.sum(line, axis=1)
    found = values[...]
    folded = jnp.concatenate([found, pltpu.roll(found, 64, axis=1)], axis=0)
    pay_ref[...] = jnp.zeros(pay_ref.shape, F32)
    start = pl.multiple_of((1 - panel_ref[0]) * 64, 64)
    pay_ref[pl.ds(start, 64), :] = jnp.transpose(folded)[:64, :]
    for k, c in edges:
        column(k, c).wait()


def payload_call(panel, x, base, fractions):
    stacked, cols, rows = x.shape
    tiles = base.shape[0]
    vmem = pl.BlockSpec(memory_space=pltpu.VMEM)
    anywhere = pl.BlockSpec(memory_space=pl.ANY)
    return pl.pallas_call(
        payload_kernel,
        out_shape=(
            jax.ShapeDtypeStruct((4 * tiles, LANES), F32),
            jax.ShapeDtypeStruct((4, stacked, rows), F32),
        ),
        in_specs=[pl.BlockSpec(memory_space=pltpu.SMEM), anywhere, vmem, vmem],
        out_specs=(vmem, anywhere),
        scratch_shapes=[
            pltpu.VMEM((stacked, cols, rows), F32),
            pltpu.VMEM((stacked, LANES), F32),
            pltpu.SemaphoreType.DMA((8,)),
            pltpu.SemaphoreType.DMA((4,)),
        ],
        compiler_params=pltpu.CompilerParams(vmem_limit_bytes=32 * 2**20),
        cost_estimate=pl.CostEstimate(flops=10**9, bytes_accessed=6 * 2**20, transcendentals=0),
        name="payload",
    )(panel, x, base, fractions)


def place_kernel(panel_ref, got_ref, dest_ref, border_ref):
    start = pl.multiple_of((1 - panel_ref[0]) * 64, 64)
    got = got_ref[pl.ds(start, 64), :]
    turned = jnp.transpose(jnp.concatenate([got, got], axis=0))
    lane = lax.broadcasted_iota(jnp.int32, (64, LANES), 1)
    values = jnp.where(lane < 64, turned[:64], turned[64:])
    point = lane_order(dest_ref[...].astype(F32)).astype(jnp.int32)
    placing = jnp.where(
        lax.broadcasted_iota(jnp.int32, (LANES, LANES), 0) == point, 1.0, 0.0
    ).astype(BF16)
    dims = (((1,), (1,)), ((), ()))
    high, low = halves(values)
    border = lax.dot_general(high, placing, dims, preferred_element_type=F32)
    border_ref[...] = border + lax.dot_general(low, placing, dims, preferred_element_type=F32)


def place_call(panel, got, dest):
    vmem = pl.BlockSpec(memory_space=pltpu.VMEM)
    return pl.pallas_call(
        place_kernel,
        out_shape=jax.ShapeDtypeStruct((64, LANES), F32),
        in_specs=[pl.BlockSpec(memory_space=pltpu.SMEM), vmem, vmem],
        out_specs=vmem,
        cost_estimate=pl.CostEstimate(flops=10**7, bytes_accessed=2**17, transcendentals=0),
        name="place",
    )(panel, got, dest)


def section_chunk(load, scale, lane):
    a_r, a_t, a_p, c_r, c_t, c_p = scale
    c_mid = 2.0 * c_r + 30.0 * c_t + 30.0 * c_p

    def parts(f, laplace=True):
        x = load(f, 0, 0, 0)
        left, right = load(f, 0, 0, -1), load(f, 0, 0, 1)
        inner, outer = load(f, -1, 0, 0), load(f, 1, 0, 0)
        t1 = pltpu.roll(jnp.where(lane < 1, right, x), LANES - 1, axis=1)
        t2 = pltpu.roll(jnp.where(lane < 2, right, x), LANES - 2, axis=1)
        s1 = pltpu.roll(jnp.where(lane >= LANES - 1, left, x), 1, axis=1)
        s2 = pltpu.roll(jnp.where(lane >= LANES - 2, left, x), 2, axis=1)
        p1, p2 = load(f, 0, 1, 0), load(f, 0, 2, 0)
        q1, q2 = load(f, 0, -1, 0), load(f, 0, -2, 0)
        g_r = outer - inner
        g_t = 8.0 * (t1 - s1) - (t2 - s2)
        g_p = 8.0 * (p1 - q1) - (p2 - q2)
        if not laplace:
            return x, g_r, g_t, g_p, None
        lap = c_r * (outer + inner) + c_t * (16.0 * (t1 + s1) - (t2 + s2))
        lap = lap + c_p * (16.0 * (p1 + q1) - (p2 + q2)) - c_mid * x
        return x, g_r, g_t, g_p, lap

    vel = tuple(load(1 + i, 0, 0, 0) * a for i, a in enumerate((a_r, a_t, a_p)))
    mag = tuple(load(4 + i, 0, 0, 0) * a for i, a in enumerate((a_r, a_t, a_p)))

    def along(v, g):
        return v[0] * g[0] + v[1] * g[1] + v[2] * g[2]

    new = [None] * 8
    rho, *g_rho, _ = parts(0, laplace=False)
    inv_rho = jnp.exp(-rho)
    rho_adv = along(vel, g_rho)
    pres, *g_pres, lap = parts(7)
    part_pres = pres - along(vel, g_pres) + 0.3 * lap
    div = None
    part_mag = []
    for i, a in enumerate((a_r, a_t, a_p)):
        u, *g_u, lap_u = parts(1 + i)
        b, *g_b, lap_b = parts(4 + i)
        term = a * g_u[i]
        div = term if div is None else div + term
        force = along(mag, g_b) - a * g_pres[i]
        new[1 + i] = u - along(vel, g_u) + inv_rho * force + 0.25 * lap_u
        part_mag.append((b, b - along(vel, g_b) + along(mag, g_u) + 0.2 * lap_b))
    for i, (b, part) in enumerate(part_mag):
        new[4 + i] = part - b * div
    new[0] = rho - rho_adv - div
    new[7] = part_pres - (5.0 / 3.0) * pres * div
    return new


def section_kernel(tiles_here, merge, shells, cols, rows, phi_count, *refs):
    if merge:
        inverse_ref, sine_ref, x_ref, below_ref, above_ref, before_ref, after_ref, *refs = refs
        own_ref, low_ref, high_ref, left_ref, right_ref, _, out_ref, *refs = refs
        held, made, split, spread, in_sem, halo_sem, out_sem = refs
    else:
        inverse_ref, sine_ref, x_ref, below_ref, above_ref, before_ref, after_ref, *refs = refs
        out_ref, held, made, in_sem, halo_sem, out_sem = refs
    lane_tiles = rows // LANES
    fields = 8
    theta_step, phi_step, shell_step, spacing = geometry(rows, phi_count)
    step = 0.2 * spacing

    def loads(s, k):
        lanes = pl.ds(k * LANES, LANES)
        if isinstance(s, int) and s == -1:
            source = below_ref.at[:, :, lanes]
        elif isinstance(s, int) and s == shells:
            source = above_ref.at[:, :, lanes]
        else:
            source = x_ref.at[:, s, :, lanes]
        target = held.at[k, :, s + 1, pl.ds(FIRST, cols), :]
        return pltpu.make_async_copy(source, target, in_sem.at[s + 1, k])

    def halo(side, c, k):
        source = (before_ref, after_ref)[side]
        row = (FIRST - 2, FIRST + cols)[side] + c
        return pltpu.make_async_copy(
            source.at[c, :, :, pl.ds(k * LANES, LANES)],
            held.at[k, :, pl.ds(1, shells), row, :],
            halo_sem.at[side, c, k],
        )

    def store(s, n, k):
        return pltpu.make_async_copy(
            made.at[n, s], out_ref.at[:, s, :, pl.ds(k * LANES, LANES)], out_sem.at[n, s]
        )

    halos = [(side, c, k) for side in range(2) for c in range(2) for k in tiles_here]
    for h in halos:
        halo(*h).start()
    for s in range(-1, shells + 1):
        for k in range(lane_tiles):
            loads(s, k).start()

    lane = lax.broadcasted_iota(jnp.int32, (8, LANES), 1)

    if merge:
        for n, ref in enumerate((own_ref, low_ref, high_ref, left_ref, right_ref)):
            value = ref[...]
            high = value.astype(BF16).astype(F32)
            split[n, 0] = high
            split[n, 1] = value - high
        wide = lax.broadcasted_iota(jnp.int32, (LANES, LANES), 1)
        group = lax.broadcasted_iota(jnp.int32, (LANES, LANES), 0) // cols
        target = jnp.where(group < 2, group, LANES - 4 + group)
        spreading = jnp.where(wide == target, 1.0, 0.0).astype(BF16)
        row = lax.broadcasted_iota(jnp.int32, (8, LANES), 0)
        within = lane % cols

        def spread_rows(part, s, f, r, inside):
            index = pl.ds(f * shells + s, 1)
            if not inside:
                which = 1 if inside is None else 2
                return jnp.where(within == row + (8 * r - FIRST), split[which, part, index, :], 0.0)
            if r == 0:
                wanted, which = (row >= 6) & (within == row + (cols - 8)), 3
            elif r == ROWS // 8 - 1:
                wanted, which = (row < 2) & (within == row), 4
            else:
                wanted, which = within == row + (8 * r - FIRST), 0
            return jnp.where(wanted, split[which, part, index, :], 0.0)

        def merge_shell(slot, s, inside):
            tiles = range(ROWS // 8) if inside else range(1, ROWS // 8 - 1)
            for f in range(fields):
                for part in range(2):
                    block = [spread_rows(part, s, f, r, inside) for r in tiles]
                    line = jnp.concatenate(block, axis=0).astype(BF16)
                    size = 8 * len(block)
                    spread[part, f * size : (f + 1) * size, :] = line
            total = fields * 8 * len(tiles)
            out = jnp.dot(spread[0, :total], spreading, preferred_element_type=F32)
            out = out + jnp.dot(spread[1, :total], spreading, preferred_element_type=F32)
            out = out.reshape(fields, len(tiles), 8, LANES)
            for f in range(fields):
                for n, r in enumerate(tiles):
                    at = pl.ds(8 * r, 8)
                    block = out[f, n]
                    held[0, f, slot, at, :] = jnp.where(lane < 2, block, held[0, f, slot, at, :])
                    last = lane_tiles - 1
                    held[last, f, slot, at, :] = jnp.where(
                        lane >= LANES - 2, block, held[last, f, slot, at, :]
                    )

    def arrive(s):
        for k in range(lane_tiles):
            loads(s, k).wait()

    for h in halos:
        halo(*h).wait()
    arrive(-1)
    arrive(0)
    if merge:
        merge_shell(0, shells - 1, None)
        merge_shell(1, 0, True)

    def shell(s, last):
        if last:
            arrive(shells)
            if merge:
                merge_shell(shells + 1, 0, False)
        else:
            arrive(s + 1)
            if merge:
                merge_shell(s + 2, s + 1, True)
        inverse = inverse_ref[s]
        a_r = step * 0.5 / shell_step
        a_t = (step / (12.0 * theta_step)) * inverse
        c_r = step * spacing / (shell_step * shell_step)
        c_t = (step * spacing / (12.0 * theta_step * theta_step)) * (inverse * inverse)
        for n, k in enumerate(tiles_here):
            over = sine_ref[k : k + 1, :] * inverse
            a_p = jnp.broadcast_to((step / (12.0 * phi_step)) * over, (8, LANES))
            c_p = jnp.broadcast_to(
                (step * spacing / (12.0 * phi_step * phi_step)) * (over * over), (8, LANES)
            )
            for c in range(cols // 8):

                def load(f, ds, dc, dk):
                    if not 0 <= k + dk < lane_tiles:
                        return jnp.zeros((8, LANES), F32)
                    return held[k + dk, f, s + 1 + ds, FIRST + 8 * c + dc : FIRST + 8 * c + dc + 8, :]

                new = section_chunk(load, (a_r, a_t, a_p, c_r, c_t, c_p), lane)
                for f in range(fields):
                    made[n, s, f, 8 * c : 8 * c + 8, :] = new[f]
            store(s, n, k).start()

    @pl.loop(0, shells - 1)
    def _(s):
        shell(s, False)

    shell(shells - 1, True)
    for s in range(shells):
        for n, k in enumerate(tiles_here):
            store(s, n, k).wait()


def section_call(tiles_here, inverse, sine, x, faces, halos, borders=None, before=None):
    fields, shells, cols, rows = x.shape
    merge = borders is not None
    lane_tiles = rows // LANES
    vmem = pl.BlockSpec(memory_space=pltpu.VMEM)
    anywhere = pl.BlockSpec(memory_space=pl.ANY)
    operands = [inverse, sine, x, *faces, *halos]
    specs = [pl.BlockSpec(memory_space=pltpu.SMEM), vmem] + [anywhere] * 5
    scratch = [
        pltpu.VMEM((lane_tiles, fields, shells + 2, ROWS, LANES), F32),
        pltpu.VMEM((len(tiles_here), shells, fields, cols, LANES), F32),
    ]
    aliases = {}
    if merge:
        operands += [*borders, before]
        specs += [vmem] * 5 + [anywhere]
        aliases = {len(operands) - 1: 0}
        scratch += [
            pltpu.VMEM((5, 2, fields * shells, LANES), F32),
            pltpu.VMEM((2, fields * ROWS, LANES), BF16),
        ]
    scratch += [
        pltpu.SemaphoreType.DMA((shells + 2, lane_tiles)),
        pltpu.SemaphoreType.DMA((2, 2, lane_tiles)),
        pltpu.SemaphoreType.DMA((len(tiles_here), shells)),
    ]
    phi_count = cols * lax.axis_size("tile")
    return pl.pallas_call(
        functools.partial(
            section_kernel, tuple(tiles_here), merge, shells, cols, rows, phi_count
        ),
        out_shape=jax.ShapeDtypeStruct(x.shape, F32),
        in_specs=specs,
        out_specs=anywhere,
        scratch_shapes=scratch,
        input_output_aliases=aliases,
        compiler_params=pltpu.CompilerParams(vmem_limit_bytes=40 * 2**20),
        cost_estimate=pl.CostEstimate(
            flops=2 * 10**8, bytes_accessed=8 * 2**20, transcendentals=10**5
        ),
        name="border_tiles" if merge else "inner_tiles",
    )(*operands)


def shifted(x, axis, by):
    peers = lax.axis_size(axis)
    route = [(i, i + by) for i in range(peers) if 0 <= i + by < peers]
    return lax.ppermute(x, axis, route)


def on_device(state, donor_base, fractions, dest_pos):
    x = state[0]
    fields, shells, cols, rows = x.shape
    tiles = lax.axis_size("tile")
    theta_step, phi_step, shell_step, spacing = geometry(rows, cols * tiles)
    panel = lax.axis_index("panel").astype(jnp.int32).reshape(1)

    below = shifted(x[:, shells - 1], "rad", 1)
    above = shifted(x[:, 0], "rad", -1)

    payload, edge_cols = payload_call(
        panel, x.reshape(fields * shells, cols, rows), donor_base[0, 0], fractions[0, 0]
    )
    edge_cols = edge_cols.reshape(4, fields, shells, rows)
    before = shifted(edge_cols[2:], "tile", 1)
    after = shifted(edge_cols[:2], "tile", -1)

    got = lax.all_to_all(payload, ("panel", "tile"), split_axis=0, concat_axis=0, tiled=True)

    colat = 0.25 * math.pi + (np.arange(rows) + 0.5) * theta_step
    sine = jnp.asarray((1.0 / np.sin(colat)).reshape(-1, LANES), F32)
    layers = lax.axis_size("rad") * shells
    radius = BASE_RADIUS + (np.arange(layers) + 0.5) * shell_step
    inverse = lax.dynamic_slice_in_dim(
        jnp.asarray(1.0 / radius, F32), lax.axis_index("rad") * shells, shells
    )
    lane_tiles = rows // LANES
    inner = tuple(range(1, lane_tiles - 1))
    outer = (0, lane_tiles - 1)
    faces, halos = (below, above), (before, after)
    first = section_call(inner, inverse, sine, x, faces, halos)

    border = place_call(panel, got, dest_pos[0, 0])
    borders = (
        border,
        shifted(border, "rad", 1),
        shifted(border, "rad", -1),
        shifted(border, "tile", 1),
        shifted(border, "tile", -1),
    )
    updated = section_call(outer, inverse, sine, x, faces, halos, borders, first)
    return updated[None]


def solution(mesh):
    placed = (
        P("panel", None, "rad", "tile", None),
        P("panel", "tile", None, None),
        P("panel", "tile", None, None, None),
        P("panel", "tile", None, None),
    )
    return jax.shard_map(
        on_device,
        mesh=mesh,
        in_specs=placed,
        out_specs=P("panel", None, "rad", "tile", None),
        check_vma=False,
    )
```

time: 138 us -> 76.4 us (0.55)
  the two profiles are of different devices: /device:TPU:4 before, /device:TPU:25 now
where the time goes in v1:
time: 76.4 us; the launch traced here: 76 us
  starting transfers between devices  39.2 us (51%)
  Pallas kernels  20.3 us (27%)
  local copies, waits for them, and re-layouts  8.82 us (12%)
  waiting for transfers between devices  7.4 us (10%)
    ppermute x8, starting transfers between devices, shifted(): return lax.ppermute(x, axis, route)  27.7 us
    pallas_call x2, Pallas kernels, section_call(): pl.pallas_call(functools.partial(section_kernel, tuple(tiles_here), merge...  14.3 us
    all_to_all x1, starting transfers between devices, on_device(): lax.all_to_all(payload, ('panel', 'tile'), split_axis=0, concat_axis=0, t...  11.5 us
    unnamed x20, local copies, waits for them, and re-layouts  7.84 us
    all_to_all x1, waiting for transfers between devices, on_device(): lax.all_to_all(payload, ('panel', 'tile'), split_axis=0, concat_axis=0, t...  7.38 us
    pallas_call x1, Pallas kernels, payload_call(): pl.pallas_call(payload_kernel, out_shape=(jax.ShapeDtypeStruct((4 * tiles...  4.29 us
    pallas_call x1, Pallas kernels, place_call(): pl.pallas_call(place_kernel, out_shape=jax.ShapeDtypeStruct((64, LANES),...  1.71 us
  transfers between devices with their start and end apart: 9, of which 1 were waited for; matrix products, arithmetic and copies ran while one was open for 1% of the time, Pallas kernels for 17%

profile of v1, /device:TPU:25, one launch (start us, length us, event | category | flops | bytes accessed | tf_op | source)
XLA Modules:
  0.0 76.0 jit_solution(12809382678563221254)
XLA Ops:
  0.0 0.0 copy-start.6
  0.0 0.0 copy-start.5
  0.0 2.7 %copy.16 = f32[1,8,8,32,512]{4,3,1,2,0:T(8,128)S(1)} copy(f32[1,8,8,32,512]{4,3,2,1,0:T(8,128)} %param.6) | data formatting | bytes 8388608 | tf_op args[0]
  2.7 0.0 copy-start.7
  2.7 0.0 copy-start.8
  2.7 0.0 copy-start.3
  2.8 0.1 slice_bitcast_fusion
  2.9 1.3 %collective-permute-start.1 = (f32[8,32,512]{2,1,0:T(8,128)S(1)}, f32[8,32,512]{2,1,0:T(8,128)S(1)}, u32[]{:S(2)}, u32[]{:S(2)}) collective-permute-start(f32[8,32,512]{2,1,0:T(8,128)S(1)} %get-tuple-element.9), channel_id=1, source_target_pairs={{1,0},{2,1},{3,2},{5,4},{6,5},{7,6},{9,8},{10,9},{11,10},{13,12},{... | collective-permute-start | bytes 1572872 | tf_op jit(solution)/shard_map/ppermute | solution.py:395
  4.2 4.0 %collective-permute-start = (f32[8,32,512]{2,1,0:T(8,128)S(1)}, f32[8,32,512]{2,1,0:T(8,128)S(1)}, u32[]{:S(2)}, u32[]{:S(2)}) collective-permute-start(f32[8,32,512]{2,1,0:T(8,128)S(1)} %get-tuple-element.10), channel_id=1, source_target_pairs={{0,1},{1,2},{2,3},{4,5},{5,6},{6,7},{8,9},{9,10},{10,11},{12,13},{... | collective-permute-start | bytes 1572872 | tf_op jit(solution)/shard_map/ppermute | solution.py:395
  8.2 0.0 copy-done.6
  8.2 0.1 copy.10.base_ref
  8.3 0.0 copy-done.5
  8.3 0.1 copy.9
  8.4 0.0 copy-start
  8.4 2.2 %copy-done = f32[1,8,8,32,512]{4,3,2,1,0:T(8,128)S(1)} copy-done((f32[1,8,8,32,512]{4,3,2,1,0:T(8,128)S(1)}, f32[1,8,8,32,512]{4,3,2,1,0:T(8,128)}, u32[]{:S(2)}) %copy-start) | copy-done | bytes 4194328
  10.6 4.3 %payload.1 = (f32[128,128]{1,0:T(8,128)}, f32[4,64,512]{2,1,0:T(8,128)S(1)}) custom-call(s32[1]{0:T(128)} %bitcast.4.panel_ref, f32[64,32,512]{2,1,0:T(8,128)S(1)} %bitcast.20, s32[32,4]{1,0:T(8,128)S(1)} %copy.10.base_ref, f32[2,32,4]{2,1,0:T(8,128)S(1)} %bitcast.23), custom_call_target="tpu_custom_call" | custom-call | flops 1000000000 | bytes 6291456 | tf_op jit(solution)/shard_map/payload/pallas_call | solution.py:99
  14.9 3.1 %collective-permute-start.3 = (f32[2,8,8,512]{3,2,1,0:T(8,128)S(1)}, f32[2,8,8,512]{3,2,1,0:T(8,128)S(1)}, u32[]{:S(2)}, u32[]{:S(2)}) collective-permute-start(f32[2,8,8,512]{3,2,1,0:T(8,128)S(1)} %get-tuple-element.11), channel_id=1, source_target_pairs={{4,0},{8,4},{12,8},{16,12},{20,16},{24,20},{28,24},{32,28},{36,32}... | collective-permute-start | bytes 786440 | tf_op jit(solution)/shard_map/ppermute | solution.py:395
  18.1 5.4 %collective-permute-start.2 = (f32[2,8,8,512]{3,2,1,0:T(8,128)S(1)}, f32[2,8,8,512]{3,2,1,0:T(8,128)S(1)}, u32[]{:S(2)}, u32[]{:S(2)}) collective-permute-start(f32[2,8,8,512]{3,2,1,0:T(8,128)S(1)} %get-tuple-element.12), channel_id=1, source_target_pairs={{0,4},{4,8},{8,12},{12,16},{16,20},{20,24},{24,28},{28,32},{32,36}... | collective-permute-start | bytes 786440 | tf_op jit(solution)/shard_map/ppermute | solution.py:395
  23.5 11.5 %all-to-all-start = ((f32[64,2,128]{2,1,0:T(2,128)}), f32[64,2,128]{2,1,0:T(2,128)S(1)}, u32[]{:S(2)}, u32[]{:S(2)}) async-start(f32[64,2,128]{2,1,0:T(2,128)} %bitcast.10), calls=%async_computation | async-start | bytes 131072 | tf_op jit(solution)/shard_map/all_to_all | solution.py:415
  35.0 0.0 copy-done.7
  35.0 0.7 copy.11.dest_ref
  35.7 7.4 %all-to-all-done = f32[64,2,128]{2,1,0:T(2,128)S(1)} async-done(((f32[64,2,128]{2,1,0:T(2,128)}), f32[64,2,128]{2,1,0:T(2,128)S(1)}, u32[]{:S(2)}, u32[]{:S(2)}) %all-to-all-start) | async-done | bytes 65568 | tf_op jit(solution)/shard_map/all_to_all | solution.py:415
  43.1 0.0 copy-start.4
  43.1 0.6 copy-done.4
  43.7 1.7 %place.1.refs_7_ = f32[64,128]{1,0:T(8,128)} custom-call(s32[1]{0:T(128)} %bitcast.4.panel_ref, f32[128,128]{1,0:T(8,128)} %bitcast.25, s32[32,4]{1,0:T(8,128)} %copy.11.dest_ref), custom_call_target="tpu_custom_call" | custom-call | flops 10000000 | bytes 131072 | tf_op jit(solution)/shard_map/place/pallas_call | solution.py:137
  45.4 2.3 %collective-permute-start.7 = (f32[64,128]{1,0:T(8,128)}, f32[64,128]{1,0:T(8,128)S(1)}, u32[]{:S(2)}, u32[]{:S(2)}) collective-permute-start(f32[64,128]{1,0:T(8,128)} %place.1.refs_7_), channel_id=1, source_target_pairs={{4,0},{8,4},{12,8},{16,12},{20,16},{24,20},{28,24},{32,28},{36,32}... | collective-permute-start | bytes 98312 | tf_op jit(solution)/shard_map/ppermute | solution.py:395
  47.7 0.0 collective-permute-done.3.refs_6_
  47.7 6.3 %collective-permute-start.6 = (f32[64,128]{1,0:T(8,128)}, f32[64,128]{1,0:T(8,128)S(1)}, u32[]{:S(2)}, u32[]{:S(2)}) collective-permute-start(f32[64,128]{1,0:T(8,128)} %place.1.refs_7_), channel_id=1, source_target_pairs={{0,4},{4,8},{8,12},{12,16},{16,20},{20,24},{24,28},{28,32},{32,36}... | collective-permute-start | bytes 98312 | tf_op jit(solution)/shard_map/ppermute | solution.py:395
  54.0 0.0 collective-permute-done.2.refs_5_
  54.0 1.3 %collective-permute-start.5 = (f32[64,128]{1,0:T(8,128)}, f32[64,128]{1,0:T(8,128)S(1)}, u32[]{:S(2)}, u32[]{:S(2)}) collective-permute-start(f32[64,128]{1,0:T(8,128)} %place.1.refs_7_), channel_id=1, source_target_pairs={{1,0},{2,1},{3,2},{5,4},{6,5},{7,6},{9,8},{10,9},{11,10},{13,12},{... | collective-permute-start | bytes 98312 | tf_op jit(solution)/shard_map/ppermute | solution.py:395
  55.3 0.0 collective-permute-done.1.refs_4_
  55.3 4.0 %collective-permute-start.4 = (f32[64,128]{1,0:T(8,128)}, f32[64,128]{1,0:T(8,128)S(1)}, u32[]{:S(2)}, u32[]{:S(2)}) collective-permute-start(f32[64,128]{1,0:T(8,128)} %place.1.refs_7_), channel_id=1, source_target_pairs={{0,1},{1,2},{2,3},{4,5},{5,6},{6,7},{8,9},{9,10},{10,11},{12,13},{... | collective-permute-start | bytes 98312 | tf_op jit(solution)/shard_map/ppermute | solution.py:395
  59.3 0.0 copy-done.8
  59.3 0.1 dynamic_slice.3.refs_0_
  59.4 0.0 collective-permute-done.refs_3_
  59.4 0.0 copy-done.3
  59.4 0.0 copy-start.1
  59.4 2.2 %copy-done.1 = f32[1,8,8,32,512]{4,3,2,1,0:T(8,128)S(1)} copy-done((f32[1,8,8,32,512]{4,3,2,1,0:T(8,128)S(1)}, f32[1,8,8,32,512]{4,3,2,1,0:T(8,128)}, u32[]{:S(2)}) %copy-start.1) | copy-done | bytes 4194328
  61.6 0.0 copy-start.2
  61.6 6.6 %inner_tiles.1.refs_12_ = f32[8,8,32,512]{3,2,1,0:T(8,128)} custom-call(f32[8]{0:T(128)S(1)} %dynamic_slice.3.refs_0_, f32[4,128]{1,0:T(4,128)S(1)} %copy-done.3, f32[8,8,32,512]{3,2,1,0:T(8,128)S(1)} %bitcast.21, f32[8,32,512]{2,1,0:T(8,128)S(1)} %collective-permute-done.refs_3_, f32[8,32,512]{2,1,0:T(8,128)S(1)} %collective-permute-done.1.refs_4_, ...), custom_call_target="tpu_custom_call" | custom-call | flops 200000000 | bytes 8388608 | tf_op jit(solution)/shard_map/inner_tiles/pallas_call | solution.py:375
  68.3 0.0 collective-permute-done.7.refs_11_
  68.3 0.0 collective-permute-done.6.refs_10_
  68.3 0.0 collective-permute-done.5.refs_9_
  68.3 0.0 collective-permute-done.4.refs_8_
  68.3 0.0 copy-done.2
  68.3 7.6 %border_tiles.1 = f32[8,8,32,512]{3,2,1,0:T(8,128)} custom-call(f32[8]{0:T(128)S(1)} %dynamic_slice.3.refs_0_, f32[4,128]{1,0:T(4,128)S(1)} %copy-done.3, f32[8,8,32,512]{3,2,1,0:T(8,128)S(1)} %bitcast.22, f32[8,32,512]{2,1,0:T(8,128)S(1)} %collective-permute-done.refs_3_, ...), custom_call_target="tpu_custom_call", output_to_operand_aliasing={{}: (12, {})} | custom-call | flops 200000000 | bytes 8388608 | tf_op jit(solution)/shard_map/border_tiles/pallas_call | solution.py:375
  (1 shorter events, 0.0 us)
Async XLA Ops:
  0.0 8.2 %copy-start.6 = (s32[1,1,32,4]{2,3,1,0:T(4,128)S(1)}, s32[1,1,32,4]{2,3,1,0:T(4,128)}, u32[]{:S(2)}) copy-start(s32[1,1,32,4]{2,3,1,0:T(4,128)} %param.7) | copy-start | bytes 1540
  0.0 8.3 %copy-start.5 = (f32[1,1,2,32,4]{3,4,2,1,0:T(4,128)S(1)}, f32[1,1,2,32,4]{3,4,2,1,0:T(4,128)}, u32[]{:S(2)}) copy-start(f32[1,1,2,32,4]{3,4,2,1,0:T(4,128)} %param.8) | copy-start | bytes 3076
  2.7 32.3 %copy-start.7 = (s32[1,1,32,4]{2,3,1,0:T(4,128)S(1)}, s32[1,1,32,4]{2,3,1,0:T(4,128)}, u32[]{:S(2)}) copy-start(s32[1,1,32,4]{2,3,1,0:T(4,128)} %param.9) | copy-start | bytes 1540
  2.7 56.6 %copy-start.8 = (f32[32]{0:T(128)S(1)}, f32[32]{0:T(128)}, u32[]{:S(2)}) copy-start(f32[32]{0:T(128)} %constant.21.clone) | copy-start | bytes 388
  2.7 56.7 %copy-start.3 = (f32[4,128]{1,0:T(4,128)S(1)}, f32[4,128]{1,0:T(4,128)}, u32[]{:S(2)}) copy-start(f32[4,128]{1,0:T(4,128)} %constant.20.clone.refs_1_) | copy-start | bytes 6148
  2.9 52.5 %collective-permute-start.1 = (f32[8,32,512]{2,1,0:T(8,128)S(1)}, f32[8,32,512]{2,1,0:T(8,128)S(1)}, u32[]{:S(2)}, u32[]{:S(2)}) collective-permute-start(f32[8,32,512]{2,1,0:T(8,128)S(1)} %get-tuple-element.9), channel_id=1, source_target_pairs={{1,0},{2,1},{3,2},{5,4},{6,5},{7,6},{9,8},{10,9},{11,10},{13,12},{... | collective-permute-start | bytes 1572872 | tf_op jit(solution)/shard_map/ppermute | solution.py:395
  4.2 55.2 %collective-permute-start = (f32[8,32,512]{2,1,0:T(8,128)S(1)}, f32[8,32,512]{2,1,0:T(8,128)S(1)}, u32[]{:S(2)}, u32[]{:S(2)}) collective-permute-start(f32[8,32,512]{2,1,0:T(8,128)S(1)} %get-tuple-element.10), channel_id=1, source_target_pairs={{0,1},{1,2},{2,3},{4,5},{5,6},{6,7},{8,9},{9,10},{10,11},{12,13},{... | collective-permute-start | bytes 1572872 | tf_op jit(solution)/shard_map/ppermute | solution.py:395
  8.4 2.2 %copy-start = (f32[1,8,8,32,512]{4,3,2,1,0:T(8,128)S(1)}, f32[1,8,8,32,512]{4,3,2,1,0:T(8,128)}, u32[]{:S(2)}) copy-start(f32[1,8,8,32,512]{4,3,2,1,0:T(8,128)} %param.6) | copy-start | bytes 12582916
  14.9 32.8 %collective-permute-start.3 = (f32[2,8,8,512]{3,2,1,0:T(8,128)S(1)}, f32[2,8,8,512]{3,2,1,0:T(8,128)S(1)}, u32[]{:S(2)}, u32[]{:S(2)}) collective-permute-start(f32[2,8,8,512]{3,2,1,0:T(8,128)S(1)} %get-tuple-element.11), channel_id=1, source_target_pairs={{4,0},{8,4},{12,8},{16,12},{20,16},{24,20},{28,24},{32,28},{36,32}... | collective-permute-start | bytes 786440 | tf_op jit(solution)/shard_map/ppermute | solution.py:395
  18.1 35.9 %collective-permute-start.2 = (f32[2,8,8,512]{3,2,1,0:T(8,128)S(1)}, f32[2,8,8,512]{3,2,1,0:T(8,128)S(1)}, u32[]{:S(2)}, u32[]{:S(2)}) collective-permute-start(f32[2,8,8,512]{3,2,1,0:T(8,128)S(1)} %get-tuple-element.12), channel_id=1, source_target_pairs={{0,4},{4,8},{8,12},{12,16},{16,20},{20,24},{24,28},{28,32},{32,36}... | collective-permute-start | bytes 786440 | tf_op jit(solution)/shard_map/ppermute | solution.py:395
  23.5 19.6 %all-to-all-start = ((f32[64,2,128]{2,1,0:T(2,128)}), f32[64,2,128]{2,1,0:T(2,128)S(1)}, u32[]{:S(2)}, u32[]{:S(2)}) async-start(f32[64,2,128]{2,1,0:T(2,128)} %bitcast.10), calls=%async_computation | async-start | bytes 131072 | tf_op jit(solution)/shard_map/all_to_all | solution.py:415
  43.1 0.6 copy-start.4
  45.4 22.8 %collective-permute-start.7 = (f32[64,128]{1,0:T(8,128)}, f32[64,128]{1,0:T(8,128)S(1)}, u32[]{:S(2)}, u32[]{:S(2)}) collective-permute-start(f32[64,128]{1,0:T(8,128)} %place.1.refs_7_), channel_id=1, source_target_pairs={{4,0},{8,4},{12,8},{16,12},{20,16},{24,20},{28,24},{32,28},{36,32}... | collective-permute-start | bytes 98312 | tf_op jit(solution)/shard_map/ppermute | solution.py:395
  47.7 20.5 %collective-permute-start.6 = (f32[64,128]{1,0:T(8,128)}, f32[64,128]{1,0:T(8,128)S(1)}, u32[]{:S(2)}, u32[]{:S(2)}) collective-permute-start(f32[64,128]{1,0:T(8,128)} %place.1.refs_7_), channel_id=1, source_target_pairs={{0,4},{4,8},{8,12},{12,16},{16,20},{20,24},{24,28},{28,32},{32,36}... | collective-permute-start | bytes 98312 | tf_op jit(solution)/shard_map/ppermute | solution.py:395
  54.0 14.3 %collective-permute-start.5 = (f32[64,128]{1,0:T(8,128)}, f32[64,128]{1,0:T(8,128)S(1)}, u32[]{:S(2)}, u32[]{:S(2)}) collective-permute-start(f32[64,128]{1,0:T(8,128)} %place.1.refs_7_), channel_id=1, source_target_pairs={{1,0},{2,1},{3,2},{5,4},{6,5},{7,6},{9,8},{10,9},{11,10},{13,12},{... | collective-permute-start | bytes 98312 | tf_op jit(solution)/shard_map/ppermute | solution.py:395
  55.3 13.0 %collective-permute-start.4 = (f32[64,128]{1,0:T(8,128)}, f32[64,128]{1,0:T(8,128)S(1)}, u32[]{:S(2)}, u32[]{:S(2)}) collective-permute-start(f32[64,128]{1,0:T(8,128)} %place.1.refs_7_), channel_id=1, source_target_pairs={{0,1},{1,2},{2,3},{4,5},{5,6},{6,7},{8,9},{9,10},{10,11},{12,13},{... | collective-permute-start | bytes 98312 | tf_op jit(solution)/shard_map/ppermute | solution.py:395
  59.4 2.2 %copy-start.1 = (f32[1,8,8,32,512]{4,3,2,1,0:T(8,128)S(1)}, f32[1,8,8,32,512]{4,3,2,1,0:T(8,128)}, u32[]{:S(2)}) copy-start(f32[1,8,8,32,512]{4,3,2,1,0:T(8,128)} %param.6) | copy-start | bytes 12582916
  61.6 6.7 %copy-start.2 = (f32[64,128]{1,0:T(8,128)S(1)}, f32[64,128]{1,0:T(8,128)}, u32[]{:S(2)}) copy-start(f32[64,128]{1,0:T(8,128)} %place.1.refs_7_) | copy-start | bytes 98308

commit v2 on v1

v2 whole, which is shorter than its diff:
```python
import functools
import math

import jax
import jax.numpy as jnp
import numpy as np
from jax import lax
from jax.experimental import pallas as pl
from jax.experimental.pallas import tpu as pltpu
from jax.sharding import PartitionSpec as P

BASE_RADIUS = 0.6
F32 = jnp.float32
BF16 = jnp.bfloat16
LANES = 128
FIRST = 8
ROWS = 48
PAYLOAD_VMEM = 60 * 2**20
SECTION_VMEM = 50 * 2**20
GATHER_VMEM = 50 * 2**20
SECTION_WEIGHT = 2 * 10**13
AHEAD = 4


def geometry(theta_count, phi_count):
    theta_step = 0.5 * math.pi / theta_count
    phi_step = 1.5 * math.pi / phi_count
    shell_step = 0.6 * min(theta_step, phi_step)
    corner = BASE_RADIUS * math.sin(0.25 * math.pi)
    spacing = min(shell_step, corner * theta_step, corner * phi_step)
    return (theta_step, phi_step, shell_step, spacing)


def halves(x):
    high = x.astype(BF16)
    return high, (x - high.astype(F32)).astype(BF16)


def lane_order(table):
    return jnp.concatenate([table[s : s + 1, :] for s in range(table.shape[0])], axis=1)


def turn(x):
    return jnp.transpose(jnp.concatenate([x] * (LANES // x.shape[0]), axis=0))


def stencils(base, fractions, cols, rows):
    base = lane_order(base)
    frac_theta = lane_order(fractions[0])
    frac_phi = lane_order(fractions[1])
    phi = base // rows
    theta = base - phi * rows
    position = lax.broadcasted_iota(jnp.int32, (rows, LANES), 0)
    along_theta = jnp.where(position == theta, 1.0 - frac_theta, 0.0)
    along_theta = along_theta + jnp.where(position == theta + 1, frac_theta, 0.0)
    place = lax.broadcasted_iota(jnp.int32, (cols, LANES), 0)
    along_phi = jnp.where(place == phi, 1.0 - frac_phi, 0.0)
    along_phi = along_phi + jnp.where(place == phi + 1, frac_phi, 0.0)
    return jnp.concatenate(halves(along_theta), axis=1), along_phi


def overset(block, both, along_phi):
    cols = along_phi.shape[0]
    x_high, x_low = halves(block)
    wide = jnp.dot(x_high, both, preferred_element_type=F32)
    low = jnp.dot(x_low, both[:, :LANES], preferred_element_type=F32)
    line = (wide[:, :LANES] + wide[:, LANES:] + low).reshape(-1, cols, LANES)
    return jnp.sum(line * along_phi[None], axis=1)


def edges_kernel(
    x_ref, dest_ref, up_ref, down_ref, left_ref, right_ref, faces, edges, dest_in, *sems
):
    fields, shells, cols, rows = x_ref.shape
    lane_tiles = rows // LANES
    face_sem, edge_sem, dest_sem, out_sem = sems
    points = pltpu.make_async_copy(dest_ref, dest_in, dest_sem)
    points.start()
    ends = [
        pltpu.make_async_copy(
            x_ref.at[:, (shells - 1, 0)[side], :, pl.ds(k * LANES, LANES)],
            faces.at[side, pl.ds(k * fields, fields)],
            face_sem.at[side, k],
        )
        for side in range(2)
        for k in range(lane_tiles)
    ]
    sides = [
        pltpu.make_async_copy(
            x_ref.at[:, :, (0, cols - 2)[side] + c, :],
            edges.at[side, c, pl.ds(0, fields)],
            edge_sem.at[side, c],
        )
        for side in range(2)
        for c in range(2)
    ]
    stores = [
        pltpu.make_async_copy(source, ref, out_sem.at[n])
        for n, (source, ref) in enumerate(
            (
                (faces.at[0], up_ref),
                (faces.at[1], down_ref),
                (edges.at[0], left_ref),
                (edges.at[1], right_ref),
            )
        )
    ]
    for copy in ends + sides:
        copy.start()
    points.wait()
    table = jnp.broadcast_to(lane_order(dest_in[...].astype(F32)), (shells, LANES))
    for side in range(2):
        edges[side, 0, fields, :, :LANES] = table
    for n in range(2):
        for copy in ends[n * lane_tiles : (n + 1) * lane_tiles]:
            copy.wait()
        stores[n].start()
    for n in range(2):
        for copy in sides[2 * n : 2 * n + 2]:
            copy.wait()
        stores[2 + n].start()
    for copy in stores:
        copy.wait()


def edges_call(x, dest):
    fields, shells, cols, rows = x.shape
    lane_tiles = rows // LANES
    anywhere = pl.BlockSpec(memory_space=pl.ANY)
    face = jax.ShapeDtypeStruct((lane_tiles * fields, cols, LANES), F32)
    edge = jax.ShapeDtypeStruct((2, fields + 1, shells, rows), F32)
    return pl.pallas_call(
        edges_kernel,
        out_shape=(face, face, edge, edge),
        in_specs=[anywhere] * 2,
        out_specs=(anywhere,) * 4,
        scratch_shapes=[
            pltpu.VMEM((2, *face.shape), F32),
            pltpu.VMEM((2, *edge.shape), F32),
            pltpu.VMEM(dest.shape, dest.dtype),
            pltpu.SemaphoreType.DMA((2, lane_tiles)),
            pltpu.SemaphoreType.DMA((2, 2)),
            pltpu.SemaphoreType.DMA,
            pltpu.SemaphoreType.DMA((4,)),
        ],
        compiler_params=pltpu.CompilerParams(vmem_limit_bytes=PAYLOAD_VMEM),
        cost_estimate=pl.CostEstimate(flops=10**6, bytes_accessed=2**21, transcendentals=0),
        name="edges",
    )(x, dest)


def payload_kernel(
    x_ref, base_ref, frac_ref, values_ref, held, values, base_in, frac_in, load_sem, small_sem
):
    fields, shells, cols, rows = held.shape
    smalls = [
        pltpu.make_async_copy(ref, target, small_sem.at[n])
        for n, (ref, target) in enumerate(((base_ref, base_in), (frac_ref, frac_in)))
    ]

    def load(f):
        return pltpu.make_async_copy(x_ref.at[f], held.at[f], load_sem.at[f])

    for copy in smalls:
        copy.start()
    for f in range(AHEAD):
        load(f).start()
    for copy in smalls:
        copy.wait()
    both, along_phi = stencils(base_in[...], frac_in[...], cols, rows)
    for f in range(fields):
        load(f).wait()
        if f + AHEAD < fields:
            load(f + AHEAD).start()
        block = held[f].reshape(shells * cols, rows)
        values[f * shells : (f + 1) * shells, :] = overset(block, both, along_phi)
    last = pltpu.make_async_copy(values, values_ref, small_sem.at[0])
    last.start()
    last.wait()


def payload_call(x, base, fractions):
    fields, shells, cols, rows = x.shape
    anywhere = pl.BlockSpec(memory_space=pl.ANY)
    points = jax.ShapeDtypeStruct((fields * shells, LANES), F32)
    return pl.pallas_call(
        payload_kernel,
        out_shape=points,
        in_specs=[anywhere] * 3,
        out_specs=anywhere,
        scratch_shapes=[
            pltpu.VMEM(x.shape, F32),
            pltpu.VMEM(points.shape, F32),
            pltpu.VMEM(base.shape, base.dtype),
            pltpu.VMEM(fractions.shape, F32),
            pltpu.SemaphoreType.DMA((fields,)),
            pltpu.SemaphoreType.DMA((2,)),
        ],
        compiler_params=pltpu.CompilerParams(vmem_limit_bytes=PAYLOAD_VMEM),
        cost_estimate=pl.CostEstimate(flops=10**9, bytes_accessed=6 * 2**20, transcendentals=0),
        name="payload",
    )(x, base, fractions)


def gather_kernel(
    values_ref, base_ref, frac_ref, below_ref, above_ref, out_ref, values, base, frac, faces, sem
):
    cols = faces.shape[2]
    lane_tiles = faces.shape[1] // 8
    sources = (values_ref, base_ref, frac_ref, below_ref, above_ref)
    targets = (values, base, frac, faces.at[0], faces.at[1])
    copies = [
        pltpu.make_async_copy(source, target, sem.at[n])
        for n, (source, target) in enumerate(zip(sources, targets))
    ]
    for copy in copies:
        copy.start()
    out_ref[...] = jnp.zeros(out_ref.shape, F32)
    tiles = out_ref.shape[0] // 16
    start = pl.multiple_of((1 - lax.axis_index("panel")) * (8 * tiles), 8 * tiles)
    for copy in copies[:3]:
        copy.wait()
    both, along_phi = stencils(base[...], frac[...], cols, lane_tiles * LANES)
    value = values[...]
    turned = turn(jnp.concatenate([value, pltpu.roll(value, 64, axis=1)], axis=0))
    row = lax.broadcasted_iota(jnp.int32, (tiles, LANES), 0)
    for n in range(2):
        own = turned[n * tiles : (n + 1) * tiles]
        before = jnp.where(row == 0, 0.0, pltpu.roll(own, 1, axis=0))
        after = jnp.where(row == tiles - 1, 0.0, pltpu.roll(own, tiles - 1, axis=0))
        for k, part in enumerate((own, before, after)):
            out_ref[pl.ds(start + (2 * k + n), tiles, stride=8), :] = part
    ends = []
    for side in range(2):
        copies[3 + side].wait()
        block = [
            faces[side, 8 * k : 8 * k + 8].reshape(8 * cols, LANES) for k in range(lane_tiles)
        ]
        ends.append(overset(jnp.concatenate(block, axis=1), both, along_phi))
    value = jnp.concatenate(ends, axis=0)
    parts = [value] + [pltpu.roll(value, LANES - tiles * s, axis=1) for s in range(1, 4)]
    turned = turn(jnp.concatenate(parts, axis=0))
    out_ref[pl.ds(start + 6, tiles, stride=8), :] = turned[:tiles]


def gather_call(values, base, fractions, below, above, tiles):
    vmem = pl.BlockSpec(memory_space=pltpu.VMEM)
    anywhere = pl.BlockSpec(memory_space=pl.ANY)
    return pl.pallas_call(
        gather_kernel,
        out_shape=jax.ShapeDtypeStruct((16 * tiles, LANES), F32),
        in_specs=[anywhere] * 5,
        out_specs=vmem,
        scratch_shapes=[
            pltpu.VMEM(values.shape, F32),
            pltpu.VMEM(base.shape, base.dtype),
            pltpu.VMEM(fractions.shape, F32),
            pltpu.VMEM((2, *below.shape), F32),
            pltpu.SemaphoreType.DMA((5,)),
        ],
        compiler_params=pltpu.CompilerParams(vmem_limit_bytes=GATHER_VMEM),
        cost_estimate=pl.CostEstimate(flops=10**6, bytes_accessed=2**18, transcendentals=0),
        name="gather",
    )(values, base, fractions, below, above)


def placed_points(got_ref, dest_ref, edge, split):
    tiles = got_ref.shape[0] // 8
    lane = lax.broadcasted_iota(jnp.int32, (64, LANES), 1)

    def rows(k):
        return got_ref[pl.ds(k, tiles, stride=8), :]

    def put(n, values, points):
        placing = jnp.where(
            lax.broadcasted_iota(jnp.int32, (LANES, LANES), 0) == points.astype(jnp.int32), 1.0, 0.0
        ).astype(BF16)
        dims = (((1,), (1,)), ((), ()))
        high, low = halves(values)
        count = values.shape[0]
        for part, value in enumerate((high, low)):
            split[n, part, :count, :] = lax.dot_general(
                value, placing, dims, preferred_element_type=F32
            )

    def tile_points(k):
        turned = turn(jnp.concatenate([rows(k), rows(k + 1)], axis=0))
        return jnp.where(lane < 64, turned[:64], turned[64:])

    own = lane_order(dest_ref[...].astype(F32))
    put(0, tile_points(0), own)
    turned = turn(rows(6))
    faces = turned[:16]
    for s in range(1, 4):
        faces = jnp.where(lane[:16] // tiles == s, turned[16 * s : 16 * s + 16], faces)
    put(1, faces, own)
    put(2, tile_points(2), edge[0])
    put(3, tile_points(4), edge[1])


def section_chunk(load, scale, lane):
    a_r, a_t, a_p, c_r, c_t, c_p = scale
    c_mid = 2.0 * c_r + 30.0 * c_t + 30.0 * c_p

    def parts(f, laplace=True):
        x = load(f, 0, 0, 0)
        left, right = load(f, 0, 0, -1), load(f, 0, 0, 1)
        inner, outer = load(f, -1, 0, 0), load(f, 1, 0, 0)
        t1 = pltpu.roll(jnp.where(lane < 1, right, x), LANES - 1, axis=1)
        t2 = pltpu.roll(jnp.where(lane < 2, right, x), LANES - 2, axis=1)
        s1 = pltpu.roll(jnp.where(lane >= LANES - 1, left, x), 1, axis=1)
        s2 = pltpu.roll(jnp.where(lane >= LANES - 2, left, x), 2, axis=1)
        p1, p2 = load(f, 0, 1, 0), load(f, 0, 2, 0)
        q1, q2 = load(f, 0, -1, 0), load(f, 0, -2, 0)
        g_r = outer - inner
        g_t = 8.0 * (t1 - s1) - (t2 - s2)
        g_p = 8.0 * (p1 - q1) - (p2 - q2)
        if not laplace:
            return x, g_r, g_t, g_p, None
        lap = c_r * (outer + inner) + c_t * (16.0 * (t1 + s1) - (t2 + s2))
        lap = lap + c_p * (16.0 * (p1 + q1) - (p2 + q2)) - c_mid * x
        return x, g_r, g_t, g_p, lap

    vel = tuple(load(1 + i, 0, 0, 0) * a for i, a in enumerate((a_r, a_t, a_p)))
    mag = tuple(load(4 + i, 0, 0, 0) * a for i, a in enumerate((a_r, a_t, a_p)))

    def along(v, g):
        return v[0] * g[0] + v[1] * g[1] + v[2] * g[2]

    new = [None] * 8
    rho, *g_rho, _ = parts(0, laplace=False)
    inv_rho = jnp.exp(-rho)
    rho_adv = along(vel, g_rho)
    pres, *g_pres, lap = parts(7)
    part_pres = pres - along(vel, g_pres) + 0.3 * lap
    div = None
    part_mag = []
    for i, a in enumerate((a_r, a_t, a_p)):
        u, *g_u, lap_u = parts(1 + i)
        b, *g_b, lap_b = parts(4 + i)
        term = a * g_u[i]
        div = term if div is None else div + term
        force = along(mag, g_b) - a * g_pres[i]
        new[1 + i] = u - along(vel, g_u) + inv_rho * force + 0.25 * lap_u
        part_mag.append((b, b - along(vel, g_b) + along(mag, g_u) + 0.2 * lap_b))
    for i, (b, part) in enumerate(part_mag):
        new[4 + i] = part - b * div
    new[0] = rho - rho_adv - div
    new[7] = part_pres - (5.0 / 3.0) * pres * div
    return new


def section_kernel(tiles_here, merge, cols, rows, phi_count, *refs):
    tables_ref, x_ref, before_ref, after_ref, below_ref, above_ref, *refs = refs
    fields, shells = x_ref.shape[:2]
    if merge:
        got_ref, dest_ref, _, *refs = refs
    out_ref, held, made, sides, tables, in_sem, halo_sem, small_sem, out_sem, *refs = refs
    if merge:
        got, dest, split, spread = refs
    lane_tiles = rows // LANES
    theta_step, phi_step, shell_step, spacing = geometry(rows, phi_count)
    step = 0.2 * spacing

    def loads(s):
        if isinstance(s, int) and s in (-1, shells):
            faces = below_ref if s == -1 else above_ref
            return [
                pltpu.make_async_copy(
                    faces.at[pl.ds(k * fields, fields)],
                    held.at[k, :, pl.ds((s + 1) * ROWS + FIRST, cols), :],
                    in_sem.at[s + 1, k],
                )
                for k in tiles_here
            ]
        return [
            pltpu.make_async_copy(
                x_ref.at[:, s, :, pl.ds(k * LANES, LANES)],
                held.at[k, :, pl.ds((s + 1) * ROWS + FIRST, cols), :],
                in_sem.at[s + 1, k],
            )
            for k in range(lane_tiles)
        ]

    def halo(side):
        ref = (before_ref, after_ref)[side]
        return pltpu.make_async_copy(ref, sides.at[side], halo_sem.at[side])

    def store(s, k):
        return pltpu.make_async_copy(
            made.at[k, s], out_ref.at[:, s, :, pl.ds(k * LANES, LANES)], out_sem.at[k, s]
        )

    slab = tables_ref.at[lax.axis_index("rad")]
    smalls = [pltpu.make_async_copy(slab, tables, small_sem.at[0])]
    if merge:
        start = pl.multiple_of((1 - lax.axis_index("panel")) * got.shape[0], got.shape[0])
        smalls.append(
            pltpu.make_async_copy(
                got_ref.at[pl.ds(start, got.shape[0])], got, small_sem.at[1]
            )
        )
        smalls.append(pltpu.make_async_copy(dest_ref, dest, small_sem.at[2]))
    for copy in smalls:
        copy.start()
    for side in range(2):
        halo(side).start()
    for copy in loads(-1) + loads(shells):
        copy.start()
    for s in range(AHEAD):
        for copy in loads(s):
            copy.start()
    for copy in smalls:
        copy.wait()

    lane = lax.broadcasted_iota(jnp.int32, (8, LANES), 1)

    for side in range(2):
        halo(side).wait()
    for side in range(2):
        for c in range(2):
            at = ROWS + (FIRST - 2, FIRST + cols)[side] + c
            for k in tiles_here:
                for f in range(fields):
                    held[k, f, pl.ds(at, shells, stride=ROWS), :] = sides[
                        side, c, f, :, k * LANES : (k + 1) * LANES
                    ]

    if merge:
        edge = [sides[side, 0, fields, 0:1, :LANES] for side in range(2)]
        placed_points(got, dest, edge, split)
        wide = lax.broadcasted_iota(jnp.int32, (LANES, LANES), 1)
        group = lax.broadcasted_iota(jnp.int32, (LANES, LANES), 0) // cols
        target = jnp.where(group < 2, group, LANES - 4 + group)
        spreading = jnp.where(wide == target, 1.0, 0.0).astype(BF16)
        row = lax.broadcasted_iota(jnp.int32, (8, LANES), 0)
        within = lane % cols

        def spread_rows(part, s, f, r):
            if isinstance(s, int) and s in (-1, shells):
                index = f if s == -1 else fields + f
                wanted, which = within == row + (8 * r - FIRST), 1
            else:
                index = f * shells + s
                if r == 0:
                    wanted, which = (row >= 6) & (within == row + (cols - 8)), 2
                elif r == ROWS // 8 - 1:
                    wanted, which = (row < 2) & (within == row), 3
                else:
                    wanted, which = within == row + (8 * r - FIRST), 0
            return jnp.where(wanted, split[which, part, pl.ds(index, 1), :], 0.0)

        def merge_shell(s):
            inside = not isinstance(s, int) or 0 <= s < shells
            tiles = range(ROWS // 8) if inside else range(1, ROWS // 8 - 1)
            for f in range(fields):
                for part in range(2):
                    block = [spread_rows(part, s, f, r) for r in tiles]
                    line = jnp.concatenate(block, axis=0).astype(BF16)
                    size = 8 * len(block)
                    spread[part, f * size : (f + 1) * size, :] = line
            total = fields * 8 * len(tiles)
            out = jnp.dot(spread[0, :total], spreading, preferred_element_type=F32)
            out = out + jnp.dot(spread[1, :total], spreading, preferred_element_type=F32)
            out = out.reshape(fields, len(tiles), 8, LANES)
            last = lane_tiles - 1
            for f in range(fields):
                for n, r in enumerate(tiles):
                    at = (f, pl.ds(pl.multiple_of((s + 1) * ROWS + 8 * r, 8), 8), slice(None))
                    block = out[f, n]
                    held[(0, *at)] = jnp.where(lane < 2, block, held[(0, *at)])
                    held[(last, *at)] = jnp.where(lane >= LANES - 2, block, held[(last, *at)])

    def compute(s, k):
        inverse = tables[pl.ds(8 + s, 1), :]
        over = tables[k : k + 1, :] * inverse

        def wide(row):
            return jnp.broadcast_to(row, (8, LANES))

        a_r = step * 0.5 / shell_step
        a_t = wide((step / (12.0 * theta_step)) * inverse)
        a_p = wide((step / (12.0 * phi_step)) * over)
        c_r = step * spacing / (shell_step * shell_step)
        c_t = wide((step * spacing / (12.0 * theta_step * theta_step)) * (inverse * inverse))
        c_p = wide((step * spacing / (12.0 * phi_step * phi_step)) * (over * over))

        for c in range(cols // 8):

            def load(f, ds, dc, dk):
                if not 0 <= k + dk < lane_tiles:
                    return jnp.zeros((8, LANES), F32)
                at = pl.multiple_of((s + 1 + ds) * ROWS + FIRST + 8 * c, 8)
                return held[k + dk, f, pl.ds(at + dc, 8), :]

            new = section_chunk(load, (a_r, a_t, a_p, c_r, c_t, c_p), lane)
            for f in range(fields):
                made[k, s, f, 8 * c : 8 * c + 8, :] = new[f]

        store(s, k).start()

    for s in (-1, shells):
        for copy in loads(s):
            copy.wait()
        if merge:
            merge_shell(s)

    @pl.loop(0, shells + 1)
    def _(t):
        @pl.when(t < shells)
        def _():
            @pl.when(t + AHEAD < shells)
            def _():
                for copy in loads(t + AHEAD):
                    copy.start()

            for copy in loads(t):
                copy.wait()
            if merge:
                merge_shell(t)

        @pl.when(t > 0)
        def _():
            for k in tiles_here:
                compute(t - 1, k)

    for s in range(shells):
        for k in tiles_here:
            store(s, k).wait()


def section_call(name, tiles_here, tables, x, halos, faces, found=(), before=None):
    fields, shells, cols, rows = x.shape
    lane_tiles = rows // LANES
    merge = before is not None
    anywhere = pl.BlockSpec(memory_space=pl.ANY)
    operands = [tables, x, *halos, *faces, *found]
    scratch = [
        pltpu.VMEM((lane_tiles, fields, (shells + 2) * ROWS, LANES), F32),
        pltpu.VMEM((lane_tiles, shells, fields, cols, LANES), F32),
        pltpu.VMEM((2, *halos[0].shape), F32),
        pltpu.VMEM(tables.shape[1:], F32),
        pltpu.SemaphoreType.DMA((shells + 2, lane_tiles)),
        pltpu.SemaphoreType.DMA((2,)),
        pltpu.SemaphoreType.DMA((3,)),
        pltpu.SemaphoreType.DMA((lane_tiles, shells)),
    ]
    aliases = {}
    if merge:
        aliases = {len(operands): 0}
        operands.append(before)
        got, dest = found
        scratch += [
            pltpu.VMEM((got.shape[0] // 2, LANES), F32),
            pltpu.VMEM(dest.shape, dest.dtype),
            pltpu.VMEM((4, 2, fields * shells, LANES), F32),
            pltpu.VMEM((2, fields * ROWS, LANES), BF16),
        ]
    phi_count = cols * lax.axis_size("tile")
    return pl.pallas_call(
        functools.partial(section_kernel, tiles_here, merge, cols, rows, phi_count),
        out_shape=jax.ShapeDtypeStruct(x.shape, F32),
        in_specs=[anywhere] * len(operands),
        out_specs=anywhere,
        scratch_shapes=scratch,
        input_output_aliases=aliases,
        compiler_params=pltpu.CompilerParams(vmem_limit_bytes=SECTION_VMEM),
        cost_estimate=pl.CostEstimate(
            flops=SECTION_WEIGHT, bytes_accessed=8 * 2**20, transcendentals=2**17
        ),
        name=name,
    )(*operands)


def shifted(x, axis, by):
    peers = lax.axis_size(axis)
    route = [(i, i + by) for i in range(peers) if 0 <= i + by < peers]
    return lax.ppermute(x, axis, route)


def on_device(state, donor_base, fractions, dest_pos):
    x = state[0]
    fields, shells, cols, rows = x.shape
    tiles = lax.axis_size("tile")
    theta_step, phi_step, shell_step, spacing = geometry(rows, cols * tiles)
    dest = dest_pos[0, 0].T

    base, parts = donor_base[0, 0].T, jnp.swapaxes(fractions[0, 0], 1, 2)
    up, down, left, right = edges_call(x, dest)
    faces = (shifted(up, "rad", 1), shifted(down, "rad", -1))
    halos = (shifted(right, "tile", 1), shifted(left, "tile", -1))
    values = payload_call(x, base, parts)
    sent = gather_call(values, base, parts, *faces, tiles)

    colat = 0.25 * math.pi + (np.arange(rows) + 0.5) * theta_step
    peers = lax.axis_size("rad")
    radius = BASE_RADIUS + (np.arange(peers * shells) + 0.5) * shell_step
    every = np.zeros((peers, 8 + shells, LANES), np.float32)
    every[:, : rows // LANES] = (1.0 / np.sin(colat)).reshape(1, -1, LANES)
    every[:, 8:] = (1.0 / radius).reshape(peers, shells, 1)
    tables = jnp.asarray(every)
    last = rows // LANES - 1

    got = lax.all_to_all(sent, ("panel", "tile"), split_axis=0, concat_axis=0, tiled=True)
    new = section_call("inner", tuple(range(1, last)), tables, x, halos, faces)
    new = section_call("outer", (0, last), tables, x, halos, faces, (got, dest), new)
    return new[None]


def solution(mesh):
    placed = (
        P("panel", None, "rad", "tile", None),
        P("panel", "tile", None, None),
        P("panel", "tile", None, None, None),
        P("panel", "tile", None, None),
    )
    return jax.shard_map(
        on_device,
        mesh=mesh,
        in_specs=placed,
        out_specs=P("panel", None, "rad", "tile", None),
        check_vma=False,
    )
```

time: 76.4 us -> 60.1 us (0.79)
  the two profiles are of different devices: /device:TPU:25 before, /device:TPU:4 now
where the time goes in v2:
time: 60.1 us; the launch traced here: 59 us
  Pallas kernels  25.1 us (42%)
  starting transfers between devices  20.8 us (35%)
  waiting for transfers between devices  12.3 us (20%)
  local copies, waits for them, and re-layouts  0.78 us (1%)
    pallas_call x2, Pallas kernels, section_call(): pl.pallas_call(functools.partial(section_kernel, tiles_here, merge, cols,...  16.1 us
    all_to_all x1, starting transfers between devices, on_device(): lax.all_to_all(sent, ('panel', 'tile'), split_axis=0, concat_axis=0, tile...  12.4 us
    ppermute x4, starting transfers between devices, shifted(): return lax.ppermute(x, axis, route)  8.44 us
    all_to_all x1, waiting for transfers between devices, on_device(): lax.all_to_all(sent, ('panel', 'tile'), split_axis=0, concat_axis=0, tile...  6.76 us
    ppermute x4, waiting for transfers between devices, shifted(): return lax.ppermute(x, axis, route)  5.53 us
    pallas_call x1, Pallas kernels, payload_call(): pl.pallas_call(payload_kernel, out_shape=points, in_specs=[anywhere] * 3,...  4.6 us
    pallas_call x1, Pallas kernels, edges_call(): pl.pallas_call(edges_kernel, out_shape=(face, face, edge, edge), in_specs...  2.49 us
    pallas_call x1, Pallas kernels, gather_call(): pl.pallas_call(gather_kernel, out_shape=jax.ShapeDtypeStruct((16 * tiles,...  1.87 us
  transfers between devices with their start and end apart: 5, of which 3 were waited for; matrix products, arithmetic and copies ran while one was open for 0% of the time, Pallas kernels for 23%

profile of v2, /device:TPU:4, one launch (start us, length us, event | category | flops | bytes accessed | tf_op | source)
XLA Modules:
  0.0 59.0 jit_solution(17713281540850615365)
XLA Ops:
  0.0 0.0 copy-start.1
  0.0 0.0 copy-start.2
  0.0 0.0 copy-start.4
  0.0 2.5 %edges.1 = (f32[32,32,128]{2,1,0:T(8,128)}, f32[32,32,128]{2,1,0:T(8,128)}, f32[2,9,8,512]{3,2,1,0:T(8,128)}, f32[2,9,8,512]{3,2,1,0:T(8,128)}) custom-call(f32[8,8,32,512]{3,2,1,0:T(8,128)} %bitcast.19, s32[4,32]{1,0:T(4,128)} %bitcast.17), custom_call_target="tpu_custom_call" | custom-call | flops 1000000 | bytes 2097152 | tf_op jit(solution)/shard_map/edges/pallas_call | solution.py:132
  2.5 3.1 %collective-permute-start.2 = (f32[32,32,128]{2,1,0:T(8,128)}, f32[32,32,128]{2,1,0:T(8,128)S(1)}, u32[]{:S(2)}, u32[]{:S(2)}) collective-permute-start(f32[32,32,128]{2,1,0:T(8,128)} %get-tuple-element.11), channel_id=1, source_target_pairs={{0,1},{1,2},{2,3},{4,5},{5,6},{6,7},{8,9},{9,10},{10,11},{12,13},{... | collective-permute-start | bytes 1572872 | tf_op jit(solution)/shard_map/ppermute | solution.py:578
  5.6 2.7 %collective-permute-start.3 = (f32[32,32,128]{2,1,0:T(8,128)}, f32[32,32,128]{2,1,0:T(8,128)S(1)}, u32[]{:S(2)}, u32[]{:S(2)}) collective-permute-start(f32[32,32,128]{2,1,0:T(8,128)} %get-tuple-element.12), channel_id=1, source_target_pairs={{1,0},{2,1},{3,2},{5,4},{6,5},{7,6},{9,8},{10,9},{11,10},{13,12},{... | collective-permute-start | bytes 1572872 | tf_op jit(solution)/shard_map/ppermute | solution.py:578
  8.4 1.3 %collective-permute-start = (f32[2,9,8,512]{3,2,1,0:T(8,128)}, f32[2,9,8,512]{3,2,1,0:T(8,128)S(1)}, u32[]{:S(2)}, u32[]{:S(2)}) collective-permute-start(f32[2,9,8,512]{3,2,1,0:T(8,128)} %get-tuple-element.9), channel_id=1, source_target_pairs={{0,4},{4,8},{8,12},{12,16},{16,20},{20,24},{24,28},{28,32},{32,36}... | collective-permute-start | bytes 884744 | tf_op jit(solution)/shard_map/ppermute | solution.py:578
  9.7 1.3 %collective-permute-start.1 = (f32[2,9,8,512]{3,2,1,0:T(8,128)}, f32[2,9,8,512]{3,2,1,0:T(8,128)S(1)}, u32[]{:S(2)}, u32[]{:S(2)}) collective-permute-start(f32[2,9,8,512]{3,2,1,0:T(8,128)} %get-tuple-element.10), channel_id=1, source_target_pairs={{4,0},{8,4},{12,8},{16,12},{20,16},{24,20},{28,24},{32,28},{36,32}... | collective-permute-start | bytes 884744 | tf_op jit(solution)/shard_map/ppermute | solution.py:578
  11.0 4.6 %payload.1.values_ref = f32[64,128]{1,0:T(8,128)} custom-call(f32[8,8,32,512]{3,2,1,0:T(8,128)} %bitcast.20, s32[4,32]{1,0:T(4,128)} %bitcast.15, f32[2,4,32]{2,1,0:T(4,128)} %bitcast.13), custom_call_target="tpu_custom_call" | custom-call | flops 1000000000 | bytes 6291456 | tf_op jit(solution)/shard_map/payload/pallas_call | solution.py:186
  15.6 2.7 %collective-permute-done.2.below_ref.refs_4_ = f32[32,32,128]{2,1,0:T(8,128)S(1)} collective-permute-done((f32[32,32,128]{2,1,0:T(8,128)}, f32[32,32,128]{2,1,0:T(8,128)S(1)}, u32[]{:S(2)}, u32[]{:S(2)}) %collective-permute-start.2) | collective-permute-done | bytes 524320 | tf_op jit(solution)/shard_map/ppermute | solution.py:578
  18.3 2.8 %collective-permute-done.3.above_ref.refs_5_ = f32[32,32,128]{2,1,0:T(8,128)S(1)} collective-permute-done((f32[32,32,128]{2,1,0:T(8,128)}, f32[32,32,128]{2,1,0:T(8,128)S(1)}, u32[]{:S(2)}, u32[]{:S(2)}) %collective-permute-start.3) | collective-permute-done | bytes 524320 | tf_op jit(solution)/shard_map/ppermute | solution.py:578
  21.1 0.0 copy-done.1
  21.1 0.0 copy-done.2
  21.1 0.0 copy-start
  21.1 0.8 %copy-done = f32[64,128]{1,0:T(8,128)S(1)} copy-done((f32[64,128]{1,0:T(8,128)S(1)}, f32[64,128]{1,0:T(8,128)}, u32[]{:S(2)}) %copy-start) | copy-done | bytes 32792
  21.9 1.9 %gather.1 = f32[512,128]{1,0:T(8,128)} custom-call(f32[64,128]{1,0:T(8,128)S(1)} %copy-done, s32[4,32]{1,0:T(4,128)S(1)} %bitcast.16, f32[2,4,32]{2,1,0:T(4,128)S(1)} %bitcast.14, f32[32,32,128]{2,1,0:T(8,128)S(1)} %collective-permute-done.2.below_ref.refs_4_, f32[32,32,128]{2,1,0:T(8,128)S(1)} %collective-permute-done.3.above_ref.refs_5_), custom_call_target="tpu_custom_call" | custom-call | flops 1000000 | bytes 262144 | tf_op jit(solution)/shard_map/gather/pallas_call | solution.py:249
  23.8 12.4 %all-to-all-start = ((f32[64,8,128]{2,1,0:T(8,128)}), f32[64,8,128]{2,1,0:T(8,128)}, u32[]{:S(2)}, u32[]{:S(2)}) async-start(f32[64,8,128]{2,1,0:T(8,128)} %bitcast.7), calls=%async_computation | async-start | bytes 524288 | tf_op jit(solution)/shard_map/all_to_all | solution.py:604
  36.1 0.0 collective-permute-done.refs_2_
  36.2 0.0 collective-permute-done.1.refs_3_
  36.2 0.0 copy-done.4
  36.2 0.0 copy-start.3
  36.2 7.1 %inner.1.refs_8_ = f32[8,8,32,512]{3,2,1,0:T(8,128)} custom-call(f32[4,16,128]{2,1,0:T(8,128)S(1)} %copy-done.4, f32[8,8,32,512]{3,2,1,0:T(8,128)} %bitcast.21, f32[2,9,8,512]{3,2,1,0:T(8,128)S(1)} %collective-permute-done.refs_2_, f32[2,9,8,512]{3,2,1,0:T(8,128)S(1)} %collective-permute-done.1.refs_3_, ...), custom_call_target="tpu_custom_call" | custom-call | flops 19999999655936 | bytes 8388608 | tf_op jit(solution)/shard_map/inner/pallas_call | solution.py:560
  43.3 6.8 %all-to-all-done = f32[64,8,128]{2,1,0:T(8,128)} async-done(((f32[64,8,128]{2,1,0:T(8,128)}), f32[64,8,128]{2,1,0:T(8,128)}, u32[]{:S(2)}, u32[]{:S(2)}) %all-to-all-start) | async-done | bytes 262176 | tf_op jit(solution)/shard_map/all_to_all | solution.py:604
  50.0 0.0 copy-done.3
  50.0 9.0 %outer.1 = f32[8,8,32,512]{3,2,1,0:T(8,128)} custom-call(f32[4,16,128]{2,1,0:T(8,128)S(1)} %copy-done.4, f32[8,8,32,512]{3,2,1,0:T(8,128)} %bitcast.22, f32[2,9,8,512]{3,2,1,0:T(8,128)S(1)} %collective-permute-done.refs_2_, f32[2,9,8,512]{3,2,1,0:T(8,128)S(1)} %collective-permute-done.1.refs_3_, ...), custom_call_target="tpu_custom_call", output_to_operand_aliasing={{}: (8, {})} | custom-call | flops 19999999655936 | bytes 8388608 | tf_op jit(solution)/shard_map/outer/pallas_call | solution.py:560
Async XLA Ops:
  0.0 21.1 %copy-start.1 = (f32[1,1,2,32,4]{3,4,2,1,0:T(4,128)S(1)}, f32[1,1,2,32,4]{3,4,2,1,0:T(4,128)}, u32[]{:S(2)}) copy-start(f32[1,1,2,32,4]{3,4,2,1,0:T(4,128)} %param.7) | copy-start | bytes 3076
  0.0 21.1 %copy-start.2 = (s32[1,1,32,4]{2,3,1,0:T(4,128)S(1)}, s32[1,1,32,4]{2,3,1,0:T(4,128)}, u32[]{:S(2)}) copy-start(s32[1,1,32,4]{2,3,1,0:T(4,128)} %param.6) | copy-start | bytes 1540
  0.0 36.2 %copy-start.4 = (f32[4,16,128]{2,1,0:T(8,128)S(1)}, f32[4,16,128]{2,1,0:T(8,128)}, u32[]{:S(2)}) copy-start(f32[4,16,128]{2,1,0:T(8,128)} %constant.2.clone.refs_0_) | copy-start | bytes 98308
  2.5 15.8 %collective-permute-start.2 = (f32[32,32,128]{2,1,0:T(8,128)}, f32[32,32,128]{2,1,0:T(8,128)S(1)}, u32[]{:S(2)}, u32[]{:S(2)}) collective-permute-start(f32[32,32,128]{2,1,0:T(8,128)} %get-tuple-element.11), channel_id=1, source_target_pairs={{0,1},{1,2},{2,3},{4,5},{5,6},{6,7},{8,9},{9,10},{10,11},{12,13},{... | collective-permute-start | bytes 1572872 | tf_op jit(solution)/shard_map/ppermute | solution.py:578
  5.6 15.5 %collective-permute-start.3 = (f32[32,32,128]{2,1,0:T(8,128)}, f32[32,32,128]{2,1,0:T(8,128)S(1)}, u32[]{:S(2)}, u32[]{:S(2)}) collective-permute-start(f32[32,32,128]{2,1,0:T(8,128)} %get-tuple-element.12), channel_id=1, source_target_pairs={{1,0},{2,1},{3,2},{5,4},{6,5},{7,6},{9,8},{10,9},{11,10},{13,12},{... | collective-permute-start | bytes 1572872 | tf_op jit(solution)/shard_map/ppermute | solution.py:578
  8.4 27.8 %collective-permute-start = (f32[2,9,8,512]{3,2,1,0:T(8,128)}, f32[2,9,8,512]{3,2,1,0:T(8,128)S(1)}, u32[]{:S(2)}, u32[]{:S(2)}) collective-permute-start(f32[2,9,8,512]{3,2,1,0:T(8,128)} %get-tuple-element.9), channel_id=1, source_target_pairs={{0,4},{4,8},{8,12},{12,16},{16,20},{20,24},{24,28},{28,32},{32,36}... | collective-permute-start | bytes 884744 | tf_op jit(solution)/shard_map/ppermute | solution.py:578
  9.7 26.5 %collective-permute-start.1 = (f32[2,9,8,512]{3,2,1,0:T(8,128)}, f32[2,9,8,512]{3,2,1,0:T(8,128)S(1)}, u32[]{:S(2)}, u32[]{:S(2)}) collective-permute-start(f32[2,9,8,512]{3,2,1,0:T(8,128)} %get-tuple-element.10), channel_id=1, source_target_pairs={{4,0},{8,4},{12,8},{16,12},{20,16},{24,20},{28,24},{32,28},{36,32}... | collective-permute-start | bytes 884744 | tf_op jit(solution)/shard_map/ppermute | solution.py:578
  21.1 0.8 %copy-start = (f32[64,128]{1,0:T(8,128)S(1)}, f32[64,128]{1,0:T(8,128)}, u32[]{:S(2)}) copy-start(f32[64,128]{1,0:T(8,128)} %payload.1.values_ref) | copy-start | bytes 98308
  23.8 26.3 %all-to-all-start = ((f32[64,8,128]{2,1,0:T(8,128)}), f32[64,8,128]{2,1,0:T(8,128)}, u32[]{:S(2)}, u32[]{:S(2)}) async-start(f32[64,8,128]{2,1,0:T(8,128)} %bitcast.7), calls=%async_computation | async-start | bytes 524288 | tf_op jit(solution)/shard_map/all_to_all | solution.py:604
  36.2 13.9 %copy-start.3 = (s32[1,1,32,4]{2,3,1,0:T(4,128)S(1)}, s32[1,1,32,4]{2,3,1,0:T(4,128)}, u32[]{:S(2)}) copy-start(s32[1,1,32,4]{2,3,1,0:T(4,128)} %param.8) | copy-start | bytes 1540

commit v3 on v2

--- a/solution.py
+++ b/solution.py
@@ -15,7 +15,8 @@
 LANES = 128
 FIRST = 8
 ROWS = 48
-PAYLOAD_VMEM = 60 * 2**20
+EDGES_VMEM = 60 * 2**20
+PAYLOAD_VMEM = 50 * 2**20
 SECTION_VMEM = 50 * 2**20
 GATHER_VMEM = 50 * 2**20
 SECTION_WEIGHT = 2 * 10**13
@@ -69,7 +70,7 @@
 
 
 def edges_kernel(
-    x_ref, dest_ref, up_ref, down_ref, left_ref, right_ref, faces, edges, dest_in, *sems
+    x_ref, dest_ref, near_face, far_face, near_edge, far_edge, faces, edges, dest_in, *sems
 ):
     fields, shells, cols, rows = x_ref.shape
     lane_tiles = rows // LANES
@@ -94,14 +95,16 @@
         for side in range(2)
         for c in range(2)
     ]
+    upper = lax.rem(lax.axis_index("rad"), 2)
+    second = lax.rem(lax.axis_index("tile"), 2)
     stores = [
         pltpu.make_async_copy(source, ref, out_sem.at[n])
         for n, (source, ref) in enumerate(
             (
-                (faces.at[0], up_ref),
-                (faces.at[1], down_ref),
-                (edges.at[0], left_ref),
-                (edges.at[1], right_ref),
+                (faces.at[upper], near_face),
+                (faces.at[1 - upper], far_face),
+                (edges.at[1 - second], near_edge),
+                (edges.at[second], far_edge),
             )
         )
     ]
@@ -111,14 +114,14 @@
     table = jnp.broadcast_to(lane_order(dest_in[...].astype(F32)), (shells, LANES))
     for side in range(2):
         edges[side, 0, fields, :, :LANES] = table
-    for n in range(2):
-        for copy in ends[n * lane_tiles : (n + 1) * lane_tiles]:
-            copy.wait()
-        stores[n].start()
-    for n in range(2):
-        for copy in sides[2 * n : 2 * n + 2]:
-            copy.wait()
-        stores[2 + n].start()
+    for copy in ends:
+        copy.wait()
+    for copy in stores[:2]:
+        copy.start()
+    for copy in sides:
+        copy.wait()
+    for copy in stores[2:]:
+        copy.start()
     for copy in stores:
         copy.wait()
 
@@ -143,7 +146,7 @@
             pltpu.SemaphoreType.DMA,
             pltpu.SemaphoreType.DMA((4,)),
         ],
-        compiler_params=pltpu.CompilerParams(vmem_limit_bytes=PAYLOAD_VMEM),
+        compiler_params=pltpu.CompilerParams(vmem_limit_bytes=EDGES_VMEM),
         cost_estimate=pl.CostEstimate(flops=10**6, bytes_accessed=2**21, transcendentals=0),
         name="edges",
     )(x, dest)
@@ -203,12 +206,13 @@
 
 
 def gather_kernel(
-    values_ref, base_ref, frac_ref, below_ref, above_ref, out_ref, values, base, frac, faces, sem
+    values_ref, base_ref, frac_ref, near_ref, far_ref, out_ref, values, base, frac, faces, sem
 ):
     cols = faces.shape[2]
     lane_tiles = faces.shape[1] // 8
-    sources = (values_ref, base_ref, frac_ref, below_ref, above_ref)
-    targets = (values, base, frac, faces.at[0], faces.at[1])
+    upper = lax.rem(lax.axis_index("rad"), 2)
+    sources = (values_ref, base_ref, frac_ref, near_ref, far_ref)
+    targets = (values, base, frac, faces.at[1 - upper], faces.at[upper])
     copies = [
         pltpu.make_async_copy(source, target, sem.at[n])
         for n, (source, target) in enumerate(zip(sources, targets))
@@ -231,8 +235,9 @@
         for k, part in enumerate((own, before, after)):
             out_ref[pl.ds(start + (2 * k + n), tiles, stride=8), :] = part
     ends = []
+    for copy in copies[3:]:
+        copy.wait()
     for side in range(2):
-        copies[3 + side].wait()
         block = [
             faces[side, 8 * k : 8 * k + 8].reshape(8 * cols, LANES) for k in range(lane_tiles)
         ]
@@ -243,7 +248,7 @@
     out_ref[pl.ds(start + 6, tiles, stride=8), :] = turned[:tiles]
 
 
-def gather_call(values, base, fractions, below, above, tiles):
+def gather_call(values, base, fractions, near, far, tiles):
     vmem = pl.BlockSpec(memory_space=pltpu.VMEM)
     anywhere = pl.BlockSpec(memory_space=pl.ANY)
     return pl.pallas_call(
@@ -255,13 +260,13 @@
             pltpu.VMEM(values.shape, F32),
             pltpu.VMEM(base.shape, base.dtype),
             pltpu.VMEM(fractions.shape, F32),
-            pltpu.VMEM((2, *below.shape), F32),
+            pltpu.VMEM((2, *near.shape), F32),
             pltpu.SemaphoreType.DMA((5,)),
         ],
         compiler_params=pltpu.CompilerParams(vmem_limit_bytes=GATHER_VMEM),
         cost_estimate=pl.CostEstimate(flops=10**6, bytes_accessed=2**18, transcendentals=0),
         name="gather",
-    )(values, base, fractions, below, above)
+    )(values, base, fractions, near, far)
 
 
 def placed_points(got_ref, dest_ref, edge, split):
@@ -351,7 +356,7 @@
 
 
 def section_kernel(tiles_here, merge, cols, rows, phi_count, *refs):
-    tables_ref, x_ref, before_ref, after_ref, below_ref, above_ref, *refs = refs
+    tables_ref, x_ref, near_ref, far_ref, near_face, far_face, *refs = refs
     fields, shells = x_ref.shape[:2]
     if merge:
         got_ref, dest_ref, _, *refs = refs
@@ -362,17 +367,22 @@
     theta_step, phi_step, shell_step, spacing = geometry(rows, phi_count)
     step = 0.2 * spacing
 
+    upper = lax.rem(lax.axis_index("rad"), 2)
+    second = lax.rem(lax.axis_index("tile"), 2)
+
+    def face(n):
+        ref, side = ((near_face, 1 - upper), (far_face, upper))[n]
+        at = pl.multiple_of(side * (shells + 1) * ROWS + FIRST, 8)
+        return [
+            pltpu.make_async_copy(
+                ref.at[pl.ds(k * fields, fields)],
+                held.at[k, :, pl.ds(at, cols), :],
+                in_sem.at[n * (shells + 1), k],
+            )
+            for k in tiles_here
+        ]
+
     def loads(s):
-        if isinstance(s, int) and s in (-1, shells):
-            faces = below_ref if s == -1 else above_ref
-            return [
-                pltpu.make_async_copy(
-                    faces.at[pl.ds(k * fields, fields)],
-                    held.at[k, :, pl.ds((s + 1) * ROWS + FIRST, cols), :],
-                    in_sem.at[s + 1, k],
-                )
-                for k in tiles_here
-            ]
         return [
             pltpu.make_async_copy(
                 x_ref.at[:, s, :, pl.ds(k * LANES, LANES)],
@@ -382,9 +392,9 @@
             for k in range(lane_tiles)
         ]
 
-    def halo(side):
-        ref = (before_ref, after_ref)[side]
-        return pltpu.make_async_copy(ref, sides.at[side], halo_sem.at[side])
+    def halo(n):
+        ref, side = ((near_ref, 1 - second), (far_ref, second))[n]
+        return pltpu.make_async_copy(ref, sides.at[side], halo_sem.at[n])
 
     def store(s, k):
         return pltpu.make_async_copy(
@@ -405,7 +415,7 @@
         copy.start()
     for side in range(2):
         halo(side).start()
-    for copy in loads(-1) + loads(shells):
+    for copy in face(0) + face(1):
         copy.start()
     for s in range(AHEAD):
         for copy in loads(s):
@@ -499,11 +509,11 @@
 
         store(s, k).start()
 
-    for s in (-1, shells):
-        for copy in loads(s):
-            copy.wait()
-        if merge:
-            merge_shell(s)
+    for copy in face(0) + face(1):
+        copy.wait()
+    if merge:
+        merge_shell(-1)
+        merge_shell(shells)
 
     @pl.loop(0, shells + 1)
     def _(t):
@@ -572,10 +582,9 @@
     )(*operands)
 
 
-def shifted(x, axis, by):
-    peers = lax.axis_size(axis)
-    route = [(i, i + by) for i in range(peers) if 0 <= i + by < peers]
-    return lax.ppermute(x, axis, route)
+def exchanged(x, axis, start):
+    pairs = [(i, i + 1) for i in range(start, lax.axis_size(axis) - 1, 2)]
+    return lax.ppermute(x, axis, pairs + [(j, i) for i, j in pairs])
 
 
 def on_device(state, donor_base, fractions, dest_pos):
@@ -586,9 +595,9 @@
     dest = dest_pos[0, 0].T
 
     base, parts = donor_base[0, 0].T, jnp.swapaxes(fractions[0, 0], 1, 2)
-    up, down, left, right = edges_call(x, dest)
-    faces = (shifted(up, "rad", 1), shifted(down, "rad", -1))
-    halos = (shifted(right, "tile", 1), shifted(left, "tile", -1))
+    *ends, near, far = edges_call(x, dest)
+    faces = (exchanged(ends[0], "rad", 0), exchanged(ends[1], "rad", 1))
+    halos = (exchanged(near, "tile", 0), exchanged(far, "tile", 1))
     values = payload_call(x, base, parts)
     sent = gather_call(values, base, parts, *faces, tiles)
 

time: 60.1 us -> 56.5 us (0.940); the launches traced: 59 us -> 56.3 us
  starting transfers between devices: 20.8 us -> 17.9 us
  waiting for transfers between devices: 12.3 us -> 14.2 us
  Pallas kernels: 25.1 us -> 24 us
  local copies, waits for them, and re-layouts: 0.78 us -> 0.02 us
    ppermute x4, starting transfers between devices: 8.44 us -> 5.56 us  [exchanged(): return lax.ppermute(x, axis, pairs + [(j, i) for i, j in pairs])]
    ppermute x4, waiting for transfers between devices: 5.53 us -> 7.47 us  [exchanged(): return lax.ppermute(x, axis, pairs + [(j, i) for i, j in pairs])]
    pallas_call x1, Pallas kernels: 4.6 us -> 3.68 us  [payload_call(): pl.pallas_call(payload_kernel, out_shape=points, in_specs=[anywhere] * 3,...]
    unnamed x10 -> x8, local copies, waits for them, and re-layouts: 0.78 us -> 0.02 us
  transfers between devices with their start and end apart: 5 -> 5, of which waited for: 3 -> 3; matrix products, arithmetic and copies ran while one was open for 0% -> 0% of each run, Pallas kernels for 23% -> 22%
where the time goes in v3:
time: 56.5 us; the launch traced here: 56.3 us
  Pallas kernels  24 us (42%)
  starting transfers between devices  17.9 us (32%)
  waiting for transfers between devices  14.2 us (25%)
    pallas_call x2, Pallas kernels, section_call(): pl.pallas_call(functools.partial(section_kernel, tiles_here, merge, cols,...  15.9 us
    all_to_all x1, starting transfers between devices, on_device(): lax.all_to_all(sent, ('panel', 'tile'), split_axis=0, concat_axis=0, tile...  12.4 us
    ppermute x4, waiting for transfers between devices, exchanged(): return lax.ppermute(x, axis, pairs + [(j, i) for i, j in pairs])  7.47 us
    all_to_all x1, waiting for transfers between devices, on_device(): lax.all_to_all(sent, ('panel', 'tile'), split_axis=0, concat_axis=0, tile...  6.75 us
    ppermute x4, starting transfers between devices, exchanged(): return lax.ppermute(x, axis, pairs + [(j, i) for i, j in pairs])  5.56 us
    pallas_call x1, Pallas kernels, payload_call(): pl.pallas_call(payload_kernel, out_shape=points, in_specs=[anywhere] * 3,...  3.68 us
    pallas_call x1, Pallas kernels, edges_call(): pl.pallas_call(edges_kernel, out_shape=(face, face, edge, edge), in_specs...  2.67 us
    pallas_call x1, Pallas kernels, gather_call(): pl.pallas_call(gather_kernel, out_shape=jax.ShapeDtypeStruct((16 * tiles,...  1.69 us
  transfers between devices with their start and end apart: 5, of which 3 were waited for; matrix products, arithmetic and copies ran while one was open for 0% of the time, Pallas kernels for 22%

profile of v3, /device:TPU:4, one launch (start us, length us, event | category | flops | bytes accessed | tf_op | source)
XLA Modules:
  0.0 56.3 jit_solution(5758892132952746733)
XLA Ops:
  0.0 0.0 copy-start
  0.0 0.0 copy-start.1
  0.0 0.0 copy-start.3
  0.0 2.7 %edges.1 = (f32[32,32,128]{2,1,0:T(8,128)}, f32[32,32,128]{2,1,0:T(8,128)}, f32[2,9,8,512]{3,2,1,0:T(8,128)}, f32[2,9,8,512]{3,2,1,0:T(8,128)}) custom-call(f32[8,8,32,512]{3,2,1,0:T(8,128)} %bitcast.19, s32[4,32]{1,0:T(4,128)} %bitcast.17), custom_call_target="tpu_custom_call" | custom-call | flops 1000000 | bytes 2097152 | tf_op jit(solution)/shard_map/edges/pallas_call | solution.py:135
  2.7 1.3 %collective-permute-start.2 = (f32[32,32,128]{2,1,0:T(8,128)}, f32[32,32,128]{2,1,0:T(8,128)S(1)}, u32[]{:S(2)}, u32[]{:S(2)}) collective-permute-start(f32[32,32,128]{2,1,0:T(8,128)} %get-tuple-element.11), channel_id=1, source_target_pairs={{0,1},{2,3},{1,0},{3,2},{4,5},{6,7},{5,4},{7,6},{8,9},{10,11},{9,8... | collective-permute-start | bytes 1572872 | tf_op jit(solution)/shard_map/ppermute | solution.py:587
  4.0 3.5 %collective-permute-start.3 = (f32[32,32,128]{2,1,0:T(8,128)}, f32[32,32,128]{2,1,0:T(8,128)S(1)}, u32[]{:S(2)}, u32[]{:S(2)}) collective-permute-start(f32[32,32,128]{2,1,0:T(8,128)} %get-tuple-element.12), channel_id=1, source_target_pairs={{1,2},{2,1},{5,6},{6,5},{9,10},{10,9},{13,14},{14,13},{17,18},{18,... | collective-permute-start | bytes 1572872 | tf_op jit(solution)/shard_map/ppermute | solution.py:587
  7.5 0.1 collective-permute-start
  7.6 0.7 %collective-permute-start.1 = (f32[2,9,8,512]{3,2,1,0:T(8,128)}, f32[2,9,8,512]{3,2,1,0:T(8,128)S(1)}, u32[]{:S(2)}, u32[]{:S(2)}) collective-permute-start(f32[2,9,8,512]{3,2,1,0:T(8,128)} %get-tuple-element.10), channel_id=1, source_target_pairs={{4,8},{12,16},{20,24},{28,32},{36,40},{44,48},{52,56},{60,64},{68,... | collective-permute-start | bytes 884744 | tf_op jit(solution)/shard_map/ppermute | solution.py:587
  8.3 0.0 copy-done
  8.3 0.0 copy-done.1
  8.3 3.7 %payload.1.values_ref = f32[64,128]{1,0:T(8,128)S(1)} custom-call(f32[8,8,32,512]{3,2,1,0:T(8,128)} %bitcast.20, s32[4,32]{1,0:T(4,128)S(1)} %bitcast.15, f32[2,4,32]{2,1,0:T(4,128)S(1)} %bitcast.13), custom_call_target="tpu_custom_call" | custom-call | flops 1000000000 | bytes 6291456 | tf_op jit(solution)/shard_map/payload/pallas_call | solution.py:189
  12.0 4.7 %collective-permute-done.2.near_ref.refs_4_ = f32[32,32,128]{2,1,0:T(8,128)S(1)} collective-permute-done((f32[32,32,128]{2,1,0:T(8,128)}, f32[32,32,128]{2,1,0:T(8,128)S(1)}, u32[]{:S(2)}, u32[]{:S(2)}) %collective-permute-start.2) | collective-permute-done | bytes 524320 | tf_op jit(solution)/shard_map/ppermute | solution.py:587
  16.6 2.8 %collective-permute-done.3.far_ref.refs_5_ = f32[32,32,128]{2,1,0:T(8,128)S(1)} collective-permute-done((f32[32,32,128]{2,1,0:T(8,128)}, f32[32,32,128]{2,1,0:T(8,128)S(1)}, u32[]{:S(2)}, u32[]{:S(2)}) %collective-permute-start.3) | collective-permute-done | bytes 524320 | tf_op jit(solution)/shard_map/ppermute | solution.py:587
  19.4 1.7 %gather.1 = f32[512,128]{1,0:T(8,128)} custom-call(f32[64,128]{1,0:T(8,128)S(1)} %payload.1.values_ref, s32[4,32]{1,0:T(4,128)S(1)} %bitcast.16, f32[2,4,32]{2,1,0:T(4,128)S(1)} %bitcast.14, f32[32,32,128]{2,1,0:T(8,128)S(1)} %collective-permute-done.2.near_ref.refs_4_, f32[32,32,128]{2,1,0:T(8,128)S(1)} %collective-permute-done.3.far_ref.refs_5_), custom_call_target="tpu_custom_call" | custom-call | flops 1000000 | bytes 262144 | tf_op jit(solution)/shard_map/gather/pallas_call | solution.py:254
  21.1 12.4 %all-to-all-start = ((f32[64,8,128]{2,1,0:T(8,128)}), f32[64,8,128]{2,1,0:T(8,128)}, u32[]{:S(2)}, u32[]{:S(2)}) async-start(f32[64,8,128]{2,1,0:T(8,128)} %bitcast.7), calls=%async_computation | async-start | bytes 524288 | tf_op jit(solution)/shard_map/all_to_all | solution.py:613
  33.5 0.0 collective-permute-done.refs_2_
  33.5 0.0 collective-permute-done.1.refs_3_
  33.5 0.0 copy-done.3
  33.6 0.0 copy-start.2
  33.6 7.1 %inner.1.refs_8_ = f32[8,8,32,512]{3,2,1,0:T(8,128)} custom-call(f32[4,16,128]{2,1,0:T(8,128)S(1)} %copy-done.3, f32[8,8,32,512]{3,2,1,0:T(8,128)} %bitcast.21, f32[2,9,8,512]{3,2,1,0:T(8,128)S(1)} %collective-permute-done.refs_2_, f32[2,9,8,512]{3,2,1,0:T(8,128)S(1)} %collective-permute-done.1.refs_3_, ...), custom_call_target="tpu_custom_call" | custom-call | flops 19999999655936 | bytes 8388608 | tf_op jit(solution)/shard_map/inner/pallas_call | solution.py:570
  40.7 6.8 %all-to-all-done = f32[64,8,128]{2,1,0:T(8,128)} async-done(((f32[64,8,128]{2,1,0:T(8,128)}), f32[64,8,128]{2,1,0:T(8,128)}, u32[]{:S(2)}, u32[]{:S(2)}) %all-to-all-start) | async-done | bytes 262176 | tf_op jit(solution)/shard_map/all_to_all | solution.py:613
  47.4 0.0 copy-done.2
  47.4 8.8 %outer.1 = f32[8,8,32,512]{3,2,1,0:T(8,128)} custom-call(f32[4,16,128]{2,1,0:T(8,128)S(1)} %copy-done.3, f32[8,8,32,512]{3,2,1,0:T(8,128)} %bitcast.22, f32[2,9,8,512]{3,2,1,0:T(8,128)S(1)} %collective-permute-done.refs_2_, f32[2,9,8,512]{3,2,1,0:T(8,128)S(1)} %collective-permute-done.1.refs_3_, ...), custom_call_target="tpu_custom_call", output_to_operand_aliasing={{}: (8, {})} | custom-call | flops 19999999655936 | bytes 8388608 | tf_op jit(solution)/shard_map/outer/pallas_call | solution.py:570
Async XLA Ops:
  0.0 8.3 %copy-start = (f32[1,1,2,32,4]{3,4,2,1,0:T(4,128)S(1)}, f32[1,1,2,32,4]{3,4,2,1,0:T(4,128)}, u32[]{:S(2)}) copy-start(f32[1,1,2,32,4]{3,4,2,1,0:T(4,128)} %param.7) | copy-start | bytes 3076
  0.0 8.3 %copy-start.1 = (s32[1,1,32,4]{2,3,1,0:T(4,128)S(1)}, s32[1,1,32,4]{2,3,1,0:T(4,128)}, u32[]{:S(2)}) copy-start(s32[1,1,32,4]{2,3,1,0:T(4,128)} %param.6) | copy-start | bytes 1540
  0.0 33.5 %copy-start.3 = (f32[4,16,128]{2,1,0:T(8,128)S(1)}, f32[4,16,128]{2,1,0:T(8,128)}, u32[]{:S(2)}) copy-start(f32[4,16,128]{2,1,0:T(8,128)} %constant.2.clone.refs_0_) | copy-start | bytes 98308
  2.7 14.0 %collective-permute-start.2 = (f32[32,32,128]{2,1,0:T(8,128)}, f32[32,32,128]{2,1,0:T(8,128)S(1)}, u32[]{:S(2)}, u32[]{:S(2)}) collective-permute-start(f32[32,32,128]{2,1,0:T(8,128)} %get-tuple-element.11), channel_id=1, source_target_pairs={{0,1},{2,3},{1,0},{3,2},{4,5},{6,7},{5,4},{7,6},{8,9},{10,11},{9,8... | collective-permute-start | bytes 1572872 | tf_op jit(solution)/shard_map/ppermute | solution.py:587
  4.0 15.5 %collective-permute-start.3 = (f32[32,32,128]{2,1,0:T(8,128)}, f32[32,32,128]{2,1,0:T(8,128)S(1)}, u32[]{:S(2)}, u32[]{:S(2)}) collective-permute-start(f32[32,32,128]{2,1,0:T(8,128)} %get-tuple-element.12), channel_id=1, source_target_pairs={{1,2},{2,1},{5,6},{6,5},{9,10},{10,9},{13,14},{14,13},{17,18},{18,... | collective-permute-start | bytes 1572872 | tf_op jit(solution)/shard_map/ppermute | solution.py:587
  7.5 26.0 %collective-permute-start = (f32[2,9,8,512]{3,2,1,0:T(8,128)}, f32[2,9,8,512]{3,2,1,0:T(8,128)S(1)}, u32[]{:S(2)}, u32[]{:S(2)}) collective-permute-start(f32[2,9,8,512]{3,2,1,0:T(8,128)} %get-tuple-element.9), channel_id=1, source_target_pairs={{0,4},{8,12},{16,20},{24,28},{32,36},{40,44},{48,52},{56,60},{64,6... | collective-permute-start | bytes 884744 | tf_op jit(solution)/shard_map/ppermute | solution.py:587
  7.6 26.0 %collective-permute-start.1 = (f32[2,9,8,512]{3,2,1,0:T(8,128)}, f32[2,9,8,512]{3,2,1,0:T(8,128)S(1)}, u32[]{:S(2)}, u32[]{:S(2)}) collective-permute-start(f32[2,9,8,512]{3,2,1,0:T(8,128)} %get-tuple-element.10), channel_id=1, source_target_pairs={{4,8},{12,16},{20,24},{28,32},{36,40},{44,48},{52,56},{60,64},{68,... | collective-permute-start | bytes 884744 | tf_op jit(solution)/shard_map/ppermute | solution.py:587
  21.1 26.3 %all-to-all-start = ((f32[64,8,128]{2,1,0:T(8,128)}), f32[64,8,128]{2,1,0:T(8,128)}, u32[]{:S(2)}, u32[]{:S(2)}) async-start(f32[64,8,128]{2,1,0:T(8,128)} %bitcast.7), calls=%async_computation | async-start | bytes 524288 | tf_op jit(solution)/shard_map/all_to_all | solution.py:613
  33.6 13.9 %copy-start.2 = (s32[1,1,32,4]{2,3,1,0:T(4,128)S(1)}, s32[1,1,32,4]{2,3,1,0:T(4,128)}, u32[]{:S(2)}) copy-start(s32[1,1,32,4]{2,3,1,0:T(4,128)} %param.8) | copy-start | bytes 1540

commit v4 on v3

--- a/solution.py
+++ b/solution.py
@@ -15,7 +15,8 @@
 LANES = 128
 FIRST = 8
 ROWS = 48
-EDGES_VMEM = 60 * 2**20
+FACES_VMEM = 50 * 2**20
+COLUMNS_VMEM = 60 * 2**20
 PAYLOAD_VMEM = 50 * 2**20
 SECTION_VMEM = 50 * 2**20
 GATHER_VMEM = 50 * 2**20
@@ -69,23 +70,47 @@
     return jnp.sum(line * along_phi[None], axis=1)
 
 
-def edges_kernel(
-    x_ref, dest_ref, near_face, far_face, near_edge, far_edge, faces, edges, dest_in, *sems
-):
+def faces_kernel(x_ref, near_ref, far_ref, sem):
     fields, shells, cols, rows = x_ref.shape
+    upper = lax.rem(lax.axis_index("rad"), 2)
+    copies = []
+    for n, (ref, low) in enumerate(((near_ref, upper), (far_ref, 1 - upper))):
+        s = (1 - low) * (shells - 1)
+        for k in range(rows // LANES):
+            copies.append(
+                pltpu.make_async_copy(
+                    x_ref.at[:, s, :, pl.ds(k * LANES, LANES)],
+                    ref.at[pl.ds(k * fields, fields)],
+                    sem.at[n, k],
+                )
+            )
+    for copy in copies:
+        copy.start()
+    for copy in copies:
+        copy.wait()
+
+
+def faces_call(x):
+    fields, shells, cols, rows = x.shape
     lane_tiles = rows // LANES
-    face_sem, edge_sem, dest_sem, out_sem = sems
+    anywhere = pl.BlockSpec(memory_space=pl.ANY)
+    face = jax.ShapeDtypeStruct((lane_tiles * fields, cols, LANES), F32)
+    return pl.pallas_call(
+        faces_kernel,
+        out_shape=(face, face),
+        in_specs=[anywhere],
+        out_specs=(anywhere,) * 2,
+        scratch_shapes=[pltpu.SemaphoreType.DMA((2, lane_tiles))],
+        compiler_params=pltpu.CompilerParams(vmem_limit_bytes=FACES_VMEM),
+        cost_estimate=pl.CostEstimate(flops=10**6, bytes_accessed=2**21, transcendentals=0),
+        name="faces",
+    )(x)
+
+
+def columns_kernel(x_ref, dest_ref, near_ref, far_ref, edges, dest_in, edge_sem, dest_sem, out_sem):
+    fields, shells, cols, rows = x_ref.shape
     points = pltpu.make_async_copy(dest_ref, dest_in, dest_sem)
     points.start()
-    ends = [
-        pltpu.make_async_copy(
-            x_ref.at[:, (shells - 1, 0)[side], :, pl.ds(k * LANES, LANES)],
-            faces.at[side, pl.ds(k * fields, fields)],
-            face_sem.at[side, k],
-        )
-        for side in range(2)
-        for k in range(lane_tiles)
-    ]
     sides = [
         pltpu.make_async_copy(
             x_ref.at[:, :, (0, cols - 2)[side] + c, :],
@@ -95,60 +120,45 @@
         for side in range(2)
         for c in range(2)
     ]
-    upper = lax.rem(lax.axis_index("rad"), 2)
     second = lax.rem(lax.axis_index("tile"), 2)
     stores = [
-        pltpu.make_async_copy(source, ref, out_sem.at[n])
-        for n, (source, ref) in enumerate(
-            (
-                (faces.at[upper], near_face),
-                (faces.at[1 - upper], far_face),
-                (edges.at[1 - second], near_edge),
-                (edges.at[second], far_edge),
-            )
-        )
+        pltpu.make_async_copy(edges.at[1 - second], near_ref, out_sem.at[0]),
+        pltpu.make_async_copy(edges.at[second], far_ref, out_sem.at[1]),
     ]
-    for copy in ends + sides:
+    for copy in sides:
         copy.start()
     points.wait()
     table = jnp.broadcast_to(lane_order(dest_in[...].astype(F32)), (shells, LANES))
     for side in range(2):
         edges[side, 0, fields, :, :LANES] = table
-    for copy in ends:
-        copy.wait()
-    for copy in stores[:2]:
-        copy.start()
+        edges[side, 1, fields] = jnp.zeros((shells, rows), F32)
     for copy in sides:
         copy.wait()
-    for copy in stores[2:]:
+    for copy in stores:
         copy.start()
     for copy in stores:
         copy.wait()
 
 
-def edges_call(x, dest):
+def columns_call(x, dest):
     fields, shells, cols, rows = x.shape
-    lane_tiles = rows // LANES
     anywhere = pl.BlockSpec(memory_space=pl.ANY)
-    face = jax.ShapeDtypeStruct((lane_tiles * fields, cols, LANES), F32)
     edge = jax.ShapeDtypeStruct((2, fields + 1, shells, rows), F32)
     return pl.pallas_call(
-        edges_kernel,
-        out_shape=(face, face, edge, edge),
+        columns_kernel,
+        out_shape=(edge, edge),
         in_specs=[anywhere] * 2,
-        out_specs=(anywhere,) * 4,
+        out_specs=(anywhere,) * 2,
         scratch_shapes=[
-            pltpu.VMEM((2, *face.shape), F32),
             pltpu.VMEM((2, *edge.shape), F32),
             pltpu.VMEM(dest.shape, dest.dtype),
-            pltpu.SemaphoreType.DMA((2, lane_tiles)),
             pltpu.SemaphoreType.DMA((2, 2)),
             pltpu.SemaphoreType.DMA,
-            pltpu.SemaphoreType.DMA((4,)),
+            pltpu.SemaphoreType.DMA((2,)),
         ],
-        compiler_params=pltpu.CompilerParams(vmem_limit_bytes=EDGES_VMEM),
-        cost_estimate=pl.CostEstimate(flops=10**6, bytes_accessed=2**21, transcendentals=0),
-        name="edges",
+        compiler_params=pltpu.CompilerParams(vmem_limit_bytes=COLUMNS_VMEM),
+        cost_estimate=pl.CostEstimate(flops=10**6, bytes_accessed=2**20, transcendentals=0),
+        name="columns",
     )(x, dest)
 
 
@@ -595,8 +605,9 @@
     dest = dest_pos[0, 0].T
 
     base, parts = donor_base[0, 0].T, jnp.swapaxes(fractions[0, 0], 1, 2)
-    *ends, near, far = edges_call(x, dest)
+    ends = faces_call(x)
     faces = (exchanged(ends[0], "rad", 0), exchanged(ends[1], "rad", 1))
+    near, far = columns_call(x, dest)
     halos = (exchanged(near, "tile", 0), exchanged(far, "tile", 1))
     values = payload_call(x, base, parts)
     sent = gather_call(values, base, parts, *faces, tiles)

time: 56.5 us -> 55.1 us (0.975)
  waiting for transfers between devices: 14.2 us -> 11.9 us
  Pallas kernels: 24 us -> 24.7 us
    ppermute x4, waiting for transfers between devices: 7.47 us -> 5.18 us  [exchanged(): return lax.ppermute(x, axis, pairs + [(j, i) for i, j in pairs])]
    pallas_call x1 -> x2, Pallas kernels: 2.67 us -> 3.45 us  [the longest x1 2.06 us: columns_call(): pl.pallas_call(columns_kernel, out_shape=(edge, edge), in_specs=[anywhere...]
  transfers between devices with their start and end apart: 5 -> 5, of which waited for: 3 -> 3; matrix products, arithmetic and copies ran while one was open for 0% -> 0% of each run, Pallas kernels for 22% -> 26%
where the time goes in v4:
time: 55.1 us; the launch traced here: 54.8 us
  Pallas kernels  24.7 us (45%)
  starting transfers between devices  17.9 us (32%)
  waiting for transfers between devices  11.9 us (22%)
    pallas_call x2, Pallas kernels, section_call(): pl.pallas_call(functools.partial(section_kernel, tiles_here, merge, cols,...  15.9 us
    all_to_all x1, starting transfers between devices, on_device(): lax.all_to_all(sent, ('panel', 'tile'), split_axis=0, concat_axis=0, tile...  12.4 us
    all_to_all x1, waiting for transfers between devices, on_device(): lax.all_to_all(sent, ('panel', 'tile'), split_axis=0, concat_axis=0, tile...  6.75 us
    ppermute x4, starting transfers between devices, exchanged(): return lax.ppermute(x, axis, pairs + [(j, i) for i, j in pairs])  5.56 us
    ppermute x4, waiting for transfers between devices, exchanged(): return lax.ppermute(x, axis, pairs + [(j, i) for i, j in pairs])  5.18 us
    pallas_call x1, Pallas kernels, payload_call(): pl.pallas_call(payload_kernel, out_shape=points, in_specs=[anywhere] * 3,...  3.68 us
    pallas_call x1, Pallas kernels, columns_call(): pl.pallas_call(columns_kernel, out_shape=(edge, edge), in_specs=[anywhere...  2.06 us
    pallas_call x1, Pallas kernels, gather_call(): pl.pallas_call(gather_kernel, out_shape=jax.ShapeDtypeStruct((16 * tiles,...  1.68 us
  transfers between devices with their start and end apart: 5, of which 3 were waited for; matrix products, arithmetic and copies ran while one was open for 0% of the time, Pallas kernels for 26%

profile of v4, /device:TPU:4, one launch (start us, length us, event | category | flops | bytes accessed | tf_op | source)
XLA Modules:
  0.0 54.8 jit_solution(12131133598847884448)
XLA Ops:
  0.0 0.0 copy-start
  0.0 0.0 copy-start.1
  0.0 1.4 %faces.1 = (f32[32,32,128]{2,1,0:T(8,128)S(1)}, f32[32,32,128]{2,1,0:T(8,128)S(1)}) custom-call(f32[8,8,32,512]{3,2,1,0:T(8,128)} %bitcast.19), custom_call_target="tpu_custom_call" | custom-call | flops 1000000 | bytes 2097152 | tf_op jit(solution)/shard_map/faces/pallas_call | solution.py:98
  1.4 1.3 %collective-permute-start.2 = (f32[32,32,128]{2,1,0:T(8,128)S(1)}, f32[32,32,128]{2,1,0:T(8,128)S(1)}, u32[]{:S(2)}, u32[]{:S(2)}) collective-permute-start(f32[32,32,128]{2,1,0:T(8,128)S(1)} %get-tuple-element.11), channel_id=1, source_target_pairs={{0,1},{2,3},{1,0},{3,2},{4,5},{6,7},{5,4},{7,6},{8,9},{10,11},{9,8... | collective-permute-start | bytes 1572872 | tf_op jit(solution)/shard_map/ppermute | solution.py:597
  2.7 3.5 %collective-permute-start.3 = (f32[32,32,128]{2,1,0:T(8,128)S(1)}, f32[32,32,128]{2,1,0:T(8,128)S(1)}, u32[]{:S(2)}, u32[]{:S(2)}) collective-permute-start(f32[32,32,128]{2,1,0:T(8,128)S(1)} %get-tuple-element.12), channel_id=1, source_target_pairs={{1,2},{2,1},{5,6},{6,5},{9,10},{10,9},{13,14},{14,13},{17,18},{18,... | collective-permute-start | bytes 1572872 | tf_op jit(solution)/shard_map/ppermute | solution.py:597
  6.2 0.0 copy-start.3
  6.2 2.1 %columns.1 = (f32[2,9,8,512]{3,2,1,0:T(8,128)}, f32[2,9,8,512]{3,2,1,0:T(8,128)}) custom-call(f32[8,8,32,512]{3,2,1,0:T(8,128)} %bitcast.20, s32[4,32]{1,0:T(4,128)} %bitcast.17), custom_call_target="tpu_custom_call" | custom-call | flops 1000000 | bytes 1048576 | tf_op jit(solution)/shard_map/columns/pallas_call | solution.py:147
  8.3 0.1 collective-permute-start
  8.4 0.7 %collective-permute-start.1 = (f32[2,9,8,512]{3,2,1,0:T(8,128)}, f32[2,9,8,512]{3,2,1,0:T(8,128)S(1)}, u32[]{:S(2)}, u32[]{:S(2)}) collective-permute-start(f32[2,9,8,512]{3,2,1,0:T(8,128)} %get-tuple-element.10), channel_id=1, source_target_pairs={{4,8},{12,16},{20,24},{28,32},{36,40},{44,48},{52,56},{60,64},{68,... | collective-permute-start | bytes 884744 | tf_op jit(solution)/shard_map/ppermute | solution.py:597
  9.1 0.0 copy-done
  9.1 0.0 copy-done.1
  9.1 3.7 %payload.1.values_ref = f32[64,128]{1,0:T(8,128)S(1)} custom-call(f32[8,8,32,512]{3,2,1,0:T(8,128)} %bitcast.21, s32[4,32]{1,0:T(4,128)S(1)} %bitcast.15, f32[2,4,32]{2,1,0:T(4,128)S(1)} %bitcast.13), custom_call_target="tpu_custom_call" | custom-call | flops 1000000000 | bytes 6291456 | tf_op jit(solution)/shard_map/payload/pallas_call | solution.py:199
  12.8 2.4 %collective-permute-done.2.near_ref.refs_4_ = f32[32,32,128]{2,1,0:T(8,128)S(1)} collective-permute-done((f32[32,32,128]{2,1,0:T(8,128)S(1)}, f32[32,32,128]{2,1,0:T(8,128)S(1)}, u32[]{:S(2)}, u32[]{:S(2)}) %collective-permute-start.2) | collective-permute-done | bytes 524320 | tf_op jit(solution)/shard_map/ppermute | solution.py:597
  15.2 2.8 %collective-permute-done.3.far_ref.refs_5_ = f32[32,32,128]{2,1,0:T(8,128)S(1)} collective-permute-done((f32[32,32,128]{2,1,0:T(8,128)S(1)}, f32[32,32,128]{2,1,0:T(8,128)S(1)}, u32[]{:S(2)}, u32[]{:S(2)}) %collective-permute-start.3) | collective-permute-done | bytes 524320 | tf_op jit(solution)/shard_map/ppermute | solution.py:597
  18.0 1.7 %gather.1 = f32[512,128]{1,0:T(8,128)} custom-call(f32[64,128]{1,0:T(8,128)S(1)} %payload.1.values_ref, s32[4,32]{1,0:T(4,128)S(1)} %bitcast.16, f32[2,4,32]{2,1,0:T(4,128)S(1)} %bitcast.14, f32[32,32,128]{2,1,0:T(8,128)S(1)} %collective-permute-done.2.near_ref.refs_4_, f32[32,32,128]{2,1,0:T(8,128)S(1)} %collective-permute-done.3.far_ref.refs_5_), custom_call_target="tpu_custom_call" | custom-call | flops 1000000 | bytes 262144 | tf_op jit(solution)/shard_map/gather/pallas_call | solution.py:264
  19.6 12.4 %all-to-all-start = ((f32[64,8,128]{2,1,0:T(8,128)}), f32[64,8,128]{2,1,0:T(8,128)}, u32[]{:S(2)}, u32[]{:S(2)}) async-start(f32[64,8,128]{2,1,0:T(8,128)} %bitcast.7), calls=%async_computation | async-start | bytes 524288 | tf_op jit(solution)/shard_map/all_to_all | solution.py:624
  32.0 0.0 collective-permute-done.refs_2_
  32.0 0.0 collective-permute-done.1.refs_3_
  32.0 0.0 copy-done.3
  32.1 0.0 copy-start.2
  32.1 7.1 %inner.1.refs_8_ = f32[8,8,32,512]{3,2,1,0:T(8,128)} custom-call(f32[4,16,128]{2,1,0:T(8,128)S(1)} %copy-done.3, f32[8,8,32,512]{3,2,1,0:T(8,128)} %bitcast.22, f32[2,9,8,512]{3,2,1,0:T(8,128)S(1)} %collective-permute-done.refs_2_, f32[2,9,8,512]{3,2,1,0:T(8,128)S(1)} %collective-permute-done.1.refs_3_, ...), custom_call_target="tpu_custom_call" | custom-call | flops 19999999655936 | bytes 8388608 | tf_op jit(solution)/shard_map/inner/pallas_call | solution.py:580
  39.2 6.8 %all-to-all-done = f32[64,8,128]{2,1,0:T(8,128)} async-done(((f32[64,8,128]{2,1,0:T(8,128)}), f32[64,8,128]{2,1,0:T(8,128)}, u32[]{:S(2)}, u32[]{:S(2)}) %all-to-all-start) | async-done | bytes 262176 | tf_op jit(solution)/shard_map/all_to_all | solution.py:624
  45.9 0.0 copy-done.2
  45.9 8.8 %outer.1 = f32[8,8,32,512]{3,2,1,0:T(8,128)} custom-call(f32[4,16,128]{2,1,0:T(8,128)S(1)} %copy-done.3, f32[8,8,32,512]{3,2,1,0:T(8,128)} %bitcast.23, f32[2,9,8,512]{3,2,1,0:T(8,128)S(1)} %collective-permute-done.refs_2_, f32[2,9,8,512]{3,2,1,0:T(8,128)S(1)} %collective-permute-done.1.refs_3_, ...), custom_call_target="tpu_custom_call", output_to_operand_aliasing={{}: (8, {})} | custom-call | flops 19999999655936 | bytes 8388608 | tf_op jit(solution)/shard_map/outer/pallas_call | solution.py:580
Async XLA Ops:
  0.0 9.1 %copy-start = (f32[1,1,2,32,4]{3,4,2,1,0:T(4,128)S(1)}, f32[1,1,2,32,4]{3,4,2,1,0:T(4,128)}, u32[]{:S(2)}) copy-start(f32[1,1,2,32,4]{3,4,2,1,0:T(4,128)} %param.7) | copy-start | bytes 3076
  0.0 9.1 %copy-start.1 = (s32[1,1,32,4]{2,3,1,0:T(4,128)S(1)}, s32[1,1,32,4]{2,3,1,0:T(4,128)}, u32[]{:S(2)}) copy-start(s32[1,1,32,4]{2,3,1,0:T(4,128)} %param.6) | copy-start | bytes 1540
  1.4 13.8 %collective-permute-start.2 = (f32[32,32,128]{2,1,0:T(8,128)S(1)}, f32[32,32,128]{2,1,0:T(8,128)S(1)}, u32[]{:S(2)}, u32[]{:S(2)}) collective-permute-start(f32[32,32,128]{2,1,0:T(8,128)S(1)} %get-tuple-element.11), channel_id=1, source_target_pairs={{0,1},{2,3},{1,0},{3,2},{4,5},{6,7},{5,4},{7,6},{8,9},{10,11},{9,8... | collective-permute-start | bytes 1572872 | tf_op jit(solution)/shard_map/ppermute | solution.py:597
  2.7 15.3 %collective-permute-start.3 = (f32[32,32,128]{2,1,0:T(8,128)S(1)}, f32[32,32,128]{2,1,0:T(8,128)S(1)}, u32[]{:S(2)}, u32[]{:S(2)}) collective-permute-start(f32[32,32,128]{2,1,0:T(8,128)S(1)} %get-tuple-element.12), channel_id=1, source_target_pairs={{1,2},{2,1},{5,6},{6,5},{9,10},{10,9},{13,14},{14,13},{17,18},{18,... | collective-permute-start | bytes 1572872 | tf_op jit(solution)/shard_map/ppermute | solution.py:597
  6.2 25.9 %copy-start.3 = (f32[4,16,128]{2,1,0:T(8,128)S(1)}, f32[4,16,128]{2,1,0:T(8,128)}, u32[]{:S(2)}) copy-start(f32[4,16,128]{2,1,0:T(8,128)} %constant.2.clone.refs_0_) | copy-start | bytes 98308
  8.3 23.8 %collective-permute-start = (f32[2,9,8,512]{3,2,1,0:T(8,128)}, f32[2,9,8,512]{3,2,1,0:T(8,128)S(1)}, u32[]{:S(2)}, u32[]{:S(2)}) collective-permute-start(f32[2,9,8,512]{3,2,1,0:T(8,128)} %get-tuple-element.9), channel_id=1, source_target_pairs={{0,4},{8,12},{16,20},{24,28},{32,36},{40,44},{48,52},{56,60},{64,6... | collective-permute-start | bytes 884744 | tf_op jit(solution)/shard_map/ppermute | solution.py:597
  8.4 23.7 %collective-permute-start.1 = (f32[2,9,8,512]{3,2,1,0:T(8,128)}, f32[2,9,8,512]{3,2,1,0:T(8,128)S(1)}, u32[]{:S(2)}, u32[]{:S(2)}) collective-permute-start(f32[2,9,8,512]{3,2,1,0:T(8,128)} %get-tuple-element.10), channel_id=1, source_target_pairs={{4,8},{12,16},{20,24},{28,32},{36,40},{44,48},{52,56},{60,64},{68,... | collective-permute-start | bytes 884744 | tf_op jit(solution)/shard_map/ppermute | solution.py:597
  19.6 26.3 %all-to-all-start = ((f32[64,8,128]{2,1,0:T(8,128)}), f32[64,8,128]{2,1,0:T(8,128)}, u32[]{:S(2)}, u32[]{:S(2)}) async-start(f32[64,8,128]{2,1,0:T(8,128)} %bitcast.7), calls=%async_computation | async-start | bytes 524288 | tf_op jit(solution)/shard_map/all_to_all | solution.py:624
  32.1 13.9 %copy-start.2 = (s32[1,1,32,4]{2,3,1,0:T(4,128)S(1)}, s32[1,1,32,4]{2,3,1,0:T(4,128)}, u32[]{:S(2)}) copy-start(s32[1,1,32,4]{2,3,1,0:T(4,128)} %param.8) | copy-start | bytes 1540

commit v5 on v4

--- a/solution.py
+++ b/solution.py
@@ -216,7 +216,7 @@
 
 
 def gather_kernel(
-    values_ref, base_ref, frac_ref, near_ref, far_ref, out_ref, values, base, frac, faces, sem
+    values_ref, base_ref, frac_ref, near_ref, far_ref, out_ref, values, base, frac, faces, half, sem
 ):
     cols = faces.shape[2]
     lane_tiles = faces.shape[1] // 8
@@ -229,9 +229,11 @@
     ]
     for copy in copies:
         copy.start()
-    out_ref[...] = jnp.zeros(out_ref.shape, F32)
-    tiles = out_ref.shape[0] // 16
-    start = pl.multiple_of((1 - lax.axis_index("panel")) * (8 * tiles), 8 * tiles)
+    size = half.shape[0]
+    tiles = size // 8
+    panel = lax.axis_index("panel")
+    out_ref[pl.ds(pl.multiple_of(panel * size, size), size), :] = jnp.zeros(half.shape, F32)
+    half[pl.ds(7, tiles, stride=8), :] = jnp.zeros((tiles, LANES), F32)
     for copy in copies[:3]:
         copy.wait()
     both, along_phi = stencils(base[...], frac[...], cols, lane_tiles * LANES)
@@ -243,7 +245,7 @@
         before = jnp.where(row == 0, 0.0, pltpu.roll(own, 1, axis=0))
         after = jnp.where(row == tiles - 1, 0.0, pltpu.roll(own, tiles - 1, axis=0))
         for k, part in enumerate((own, before, after)):
-            out_ref[pl.ds(start + (2 * k + n), tiles, stride=8), :] = part
+            half[pl.ds(2 * k + n, tiles, stride=8), :] = part
     ends = []
     for copy in copies[3:]:
         copy.wait()
@@ -255,7 +257,8 @@
     value = jnp.concatenate(ends, axis=0)
     parts = [value] + [pltpu.roll(value, LANES - tiles * s, axis=1) for s in range(1, 4)]
     turned = turn(jnp.concatenate(parts, axis=0))
-    out_ref[pl.ds(start + 6, tiles, stride=8), :] = turned[:tiles]
+    half[pl.ds(6, tiles, stride=8), :] = turned[:tiles]
+    out_ref[pl.ds(pl.multiple_of((1 - panel) * size, size), size), :] = half[...]
 
 
 def gather_call(values, base, fractions, near, far, tiles):
@@ -271,6 +274,7 @@
             pltpu.VMEM(base.shape, base.dtype),
             pltpu.VMEM(fractions.shape, F32),
             pltpu.VMEM((2, *near.shape), F32),
+            pltpu.VMEM((8 * tiles, LANES), F32),
             pltpu.SemaphoreType.DMA((5,)),
         ],
         compiler_params=pltpu.CompilerParams(vmem_limit_bytes=GATHER_VMEM),

time: 55.1 us -> 55.1 us (level)
  no operation moved by 1% of the time
where the time goes in v5:
time: 55.1 us; the launch traced here: 54.8 us
  Pallas kernels  24.7 us (45%)
  starting transfers between devices  17.9 us (32%)
  waiting for transfers between devices  11.9 us (22%)
    pallas_call x2, Pallas kernels, section_call(): pl.pallas_call(functools.partial(section_kernel, tiles_here, merge, cols,...  15.9 us
    all_to_all x1, starting transfers between devices, on_device(): lax.all_to_all(sent, ('panel', 'tile'), split_axis=0, concat_axis=0, tile...  12.4 us
    all_to_all x1, waiting for transfers between devices, on_device(): lax.all_to_all(sent, ('panel', 'tile'), split_axis=0, concat_axis=0, tile...  6.75 us
    ppermute x4, starting transfers between devices, exchanged(): return lax.ppermute(x, axis, pairs + [(j, i) for i, j in pairs])  5.56 us
    ppermute x4, waiting for transfers between devices, exchanged(): return lax.ppermute(x, axis, pairs + [(j, i) for i, j in pairs])  5.18 us
    pallas_call x1, Pallas kernels, payload_call(): pl.pallas_call(payload_kernel, out_shape=points, in_specs=[anywhere] * 3,...  3.68 us
    pallas_call x1, Pallas kernels, columns_call(): pl.pallas_call(columns_kernel, out_shape=(edge, edge), in_specs=[anywhere...  2.06 us
    pallas_call x1, Pallas kernels, gather_call(): pl.pallas_call(gather_kernel, out_shape=jax.ShapeDtypeStruct((16 * tiles,...  1.68 us
  transfers between devices with their start and end apart: 5, of which 3 were waited for; matrix products, arithmetic and copies ran while one was open for 0% of the time, Pallas kernels for 26%

profile of v5, /device:TPU:4, one launch (start us, length us, event | category | flops | bytes accessed | tf_op | source)
XLA Modules:
  0.0 54.8 jit_solution(15809249512407832461)
XLA Ops:
  0.0 0.0 copy-start
  0.0 0.0 copy-start.1
  0.0 1.4 %faces.1 = (f32[32,32,128]{2,1,0:T(8,128)S(1)}, f32[32,32,128]{2,1,0:T(8,128)S(1)}) custom-call(f32[8,8,32,512]{3,2,1,0:T(8,128)} %bitcast.19), custom_call_target="tpu_custom_call" | custom-call | flops 1000000 | bytes 2097152 | tf_op jit(solution)/shard_map/faces/pallas_call | solution.py:98
  1.4 1.3 %collective-permute-start.2 = (f32[32,32,128]{2,1,0:T(8,128)S(1)}, f32[32,32,128]{2,1,0:T(8,128)S(1)}, u32[]{:S(2)}, u32[]{:S(2)}) collective-permute-start(f32[32,32,128]{2,1,0:T(8,128)S(1)} %get-tuple-element.11), channel_id=1, source_target_pairs={{0,1},{2,3},{1,0},{3,2},{4,5},{6,7},{5,4},{7,6},{8,9},{10,11},{9,8... | collective-permute-start | bytes 1572872 | tf_op jit(solution)/shard_map/ppermute | solution.py:601
  2.7 3.5 %collective-permute-start.3 = (f32[32,32,128]{2,1,0:T(8,128)S(1)}, f32[32,32,128]{2,1,0:T(8,128)S(1)}, u32[]{:S(2)}, u32[]{:S(2)}) collective-permute-start(f32[32,32,128]{2,1,0:T(8,128)S(1)} %get-tuple-element.12), channel_id=1, source_target_pairs={{1,2},{2,1},{5,6},{6,5},{9,10},{10,9},{13,14},{14,13},{17,18},{18,... | collective-permute-start | bytes 1572872 | tf_op jit(solution)/shard_map/ppermute | solution.py:601
  6.2 0.0 copy-start.3
  6.2 2.1 %columns.1 = (f32[2,9,8,512]{3,2,1,0:T(8,128)}, f32[2,9,8,512]{3,2,1,0:T(8,128)}) custom-call(f32[8,8,32,512]{3,2,1,0:T(8,128)} %bitcast.20, s32[4,32]{1,0:T(4,128)} %bitcast.17), custom_call_target="tpu_custom_call" | custom-call | flops 1000000 | bytes 1048576 | tf_op jit(solution)/shard_map/columns/pallas_call | solution.py:147
  8.3 0.1 collective-permute-start
  8.4 0.7 %collective-permute-start.1 = (f32[2,9,8,512]{3,2,1,0:T(8,128)}, f32[2,9,8,512]{3,2,1,0:T(8,128)S(1)}, u32[]{:S(2)}, u32[]{:S(2)}) collective-permute-start(f32[2,9,8,512]{3,2,1,0:T(8,128)} %get-tuple-element.10), channel_id=1, source_target_pairs={{4,8},{12,16},{20,24},{28,32},{36,40},{44,48},{52,56},{60,64},{68,... | collective-permute-start | bytes 884744 | tf_op jit(solution)/shard_map/ppermute | solution.py:601
  9.1 0.0 copy-done
  9.1 0.0 copy-done.1
  9.1 3.7 %payload.1.values_ref = f32[64,128]{1,0:T(8,128)S(1)} custom-call(f32[8,8,32,512]{3,2,1,0:T(8,128)} %bitcast.21, s32[4,32]{1,0:T(4,128)S(1)} %bitcast.15, f32[2,4,32]{2,1,0:T(4,128)S(1)} %bitcast.13), custom_call_target="tpu_custom_call" | custom-call | flops 1000000000 | bytes 6291456 | tf_op jit(solution)/shard_map/payload/pallas_call | solution.py:199
  12.8 2.4 %collective-permute-done.2.near_ref.refs_4_ = f32[32,32,128]{2,1,0:T(8,128)S(1)} collective-permute-done((f32[32,32,128]{2,1,0:T(8,128)S(1)}, f32[32,32,128]{2,1,0:T(8,128)S(1)}, u32[]{:S(2)}, u32[]{:S(2)}) %collective-permute-start.2) | collective-permute-done | bytes 524320 | tf_op jit(solution)/shard_map/ppermute | solution.py:601
  15.2 2.8 %collective-permute-done.3.far_ref.refs_5_ = f32[32,32,128]{2,1,0:T(8,128)S(1)} collective-permute-done((f32[32,32,128]{2,1,0:T(8,128)S(1)}, f32[32,32,128]{2,1,0:T(8,128)S(1)}, u32[]{:S(2)}, u32[]{:S(2)}) %collective-permute-start.3) | collective-permute-done | bytes 524320 | tf_op jit(solution)/shard_map/ppermute | solution.py:601
  18.0 1.7 %gather.1 = f32[512,128]{1,0:T(8,128)} custom-call(f32[64,128]{1,0:T(8,128)S(1)} %payload.1.values_ref, s32[4,32]{1,0:T(4,128)S(1)} %bitcast.16, f32[2,4,32]{2,1,0:T(4,128)S(1)} %bitcast.14, f32[32,32,128]{2,1,0:T(8,128)S(1)} %collective-permute-done.2.near_ref.refs_4_, f32[32,32,128]{2,1,0:T(8,128)S(1)} %collective-permute-done.3.far_ref.refs_5_), custom_call_target="tpu_custom_call" | custom-call | flops 1000000 | bytes 262144 | tf_op jit(solution)/shard_map/gather/pallas_call | solution.py:267
  19.6 12.4 %all-to-all-start = ((f32[64,8,128]{2,1,0:T(8,128)}), f32[64,8,128]{2,1,0:T(8,128)}, u32[]{:S(2)}, u32[]{:S(2)}) async-start(f32[64,8,128]{2,1,0:T(8,128)} %bitcast.7), calls=%async_computation | async-start | bytes 524288 | tf_op jit(solution)/shard_map/all_to_all | solution.py:628
  32.0 0.0 collective-permute-done.refs_2_
  32.0 0.0 collective-permute-done.1.refs_3_
  32.1 0.0 copy-done.3
  32.1 0.0 copy-start.2
  32.1 7.1 %inner.1.refs_8_ = f32[8,8,32,512]{3,2,1,0:T(8,128)} custom-call(f32[4,16,128]{2,1,0:T(8,128)S(1)} %copy-done.3, f32[8,8,32,512]{3,2,1,0:T(8,128)} %bitcast.22, f32[2,9,8,512]{3,2,1,0:T(8,128)S(1)} %collective-permute-done.refs_2_, f32[2,9,8,512]{3,2,1,0:T(8,128)S(1)} %collective-permute-done.1.refs_3_, ...), custom_call_target="tpu_custom_call" | custom-call | flops 19999999655936 | bytes 8388608 | tf_op jit(solution)/shard_map/inner/pallas_call | solution.py:584
  39.2 6.8 %all-to-all-done = f32[64,8,128]{2,1,0:T(8,128)} async-done(((f32[64,8,128]{2,1,0:T(8,128)}), f32[64,8,128]{2,1,0:T(8,128)}, u32[]{:S(2)}, u32[]{:S(2)}) %all-to-all-start) | async-done | bytes 262176 | tf_op jit(solution)/shard_map/all_to_all | solution.py:628
  45.9 0.0 copy-done.2
  45.9 8.8 %outer.1 = f32[8,8,32,512]{3,2,1,0:T(8,128)} custom-call(f32[4,16,128]{2,1,0:T(8,128)S(1)} %copy-done.3, f32[8,8,32,512]{3,2,1,0:T(8,128)} %bitcast.23, f32[2,9,8,512]{3,2,1,0:T(8,128)S(1)} %collective-permute-done.refs_2_, f32[2,9,8,512]{3,2,1,0:T(8,128)S(1)} %collective-permute-done.1.refs_3_, ...), custom_call_target="tpu_custom_call", output_to_operand_aliasing={{}: (8, {})} | custom-call | flops 19999999655936 | bytes 8388608 | tf_op jit(solution)/shard_map/outer/pallas_call | solution.py:584
Async XLA Ops:
  0.0 9.1 %copy-start = (f32[1,1,2,32,4]{3,4,2,1,0:T(4,128)S(1)}, f32[1,1,2,32,4]{3,4,2,1,0:T(4,128)}, u32[]{:S(2)}) copy-start(f32[1,1,2,32,4]{3,4,2,1,0:T(4,128)} %param.7) | copy-start | bytes 3076
  0.0 9.1 %copy-start.1 = (s32[1,1,32,4]{2,3,1,0:T(4,128)S(1)}, s32[1,1,32,4]{2,3,1,0:T(4,128)}, u32[]{:S(2)}) copy-start(s32[1,1,32,4]{2,3,1,0:T(4,128)} %param.6) | copy-start | bytes 1540
  1.4 13.8 %collective-permute-start.2 = (f32[32,32,128]{2,1,0:T(8,128)S(1)}, f32[32,32,128]{2,1,0:T(8,128)S(1)}, u32[]{:S(2)}, u32[]{:S(2)}) collective-permute-start(f32[32,32,128]{2,1,0:T(8,128)S(1)} %get-tuple-element.11), channel_id=1, source_target_pairs={{0,1},{2,3},{1,0},{3,2},{4,5},{6,7},{5,4},{7,6},{8,9},{10,11},{9,8... | collective-permute-start | bytes 1572872 | tf_op jit(solution)/shard_map/ppermute | solution.py:601
  2.7 15.3 %collective-permute-start.3 = (f32[32,32,128]{2,1,0:T(8,128)S(1)}, f32[32,32,128]{2,1,0:T(8,128)S(1)}, u32[]{:S(2)}, u32[]{:S(2)}) collective-permute-start(f32[32,32,128]{2,1,0:T(8,128)S(1)} %get-tuple-element.12), channel_id=1, source_target_pairs={{1,2},{2,1},{5,6},{6,5},{9,10},{10,9},{13,14},{14,13},{17,18},{18,... | collective-permute-start | bytes 1572872 | tf_op jit(solution)/shard_map/ppermute | solution.py:601
  6.2 25.9 %copy-start.3 = (f32[4,16,128]{2,1,0:T(8,128)S(1)}, f32[4,16,128]{2,1,0:T(8,128)}, u32[]{:S(2)}) copy-start(f32[4,16,128]{2,1,0:T(8,128)} %constant.2.clone.refs_0_) | copy-start | bytes 98308
  8.3 23.8 %collective-permute-start = (f32[2,9,8,512]{3,2,1,0:T(8,128)}, f32[2,9,8,512]{3,2,1,0:T(8,128)S(1)}, u32[]{:S(2)}, u32[]{:S(2)}) collective-permute-start(f32[2,9,8,512]{3,2,1,0:T(8,128)} %get-tuple-element.9), channel_id=1, source_target_pairs={{0,4},{8,12},{16,20},{24,28},{32,36},{40,44},{48,52},{56,60},{64,6... | collective-permute-start | bytes 884744 | tf_op jit(solution)/shard_map/ppermute | solution.py:601
  8.4 23.7 %collective-permute-start.1 = (f32[2,9,8,512]{3,2,1,0:T(8,128)}, f32[2,9,8,512]{3,2,1,0:T(8,128)S(1)}, u32[]{:S(2)}, u32[]{:S(2)}) collective-permute-start(f32[2,9,8,512]{3,2,1,0:T(8,128)} %get-tuple-element.10), channel_id=1, source_target_pairs={{4,8},{12,16},{20,24},{28,32},{36,40},{44,48},{52,56},{60,64},{68,... | collective-permute-start | bytes 884744 | tf_op jit(solution)/shard_map/ppermute | solution.py:601
  19.6 26.3 %all-to-all-start = ((f32[64,8,128]{2,1,0:T(8,128)}), f32[64,8,128]{2,1,0:T(8,128)}, u32[]{:S(2)}, u32[]{:S(2)}) async-start(f32[64,8,128]{2,1,0:T(8,128)} %bitcast.7), calls=%async_computation | async-start | bytes 524288 | tf_op jit(solution)/shard_map/all_to_all | solution.py:628
  32.1 13.9 %copy-start.2 = (s32[1,1,32,4]{2,3,1,0:T(4,128)S(1)}, s32[1,1,32,4]{2,3,1,0:T(4,128)}, u32[]{:S(2)}) copy-start(s32[1,1,32,4]{2,3,1,0:T(4,128)} %param.8) | copy-start | bytes 1540

commit v6 on v5

--- a/solution.py
+++ b/solution.py
@@ -216,7 +216,7 @@
 
 
 def gather_kernel(
-    values_ref, base_ref, frac_ref, near_ref, far_ref, out_ref, values, base, frac, faces, half, sem
+    values_ref, base_ref, frac_ref, near_ref, far_ref, out_ref, values, base, frac, faces, half, blank, sem
 ):
     cols = faces.shape[2]
     lane_tiles = faces.shape[1] // 8
@@ -232,7 +232,11 @@
     size = half.shape[0]
     tiles = size // 8
     panel = lax.axis_index("panel")
-    out_ref[pl.ds(pl.multiple_of(panel * size, size), size), :] = jnp.zeros(half.shape, F32)
+    blank[...] = jnp.zeros(blank.shape, F32)
+    mine = pl.ds(pl.multiple_of(panel * size, size), size)
+    other = pl.ds(pl.multiple_of((1 - panel) * size, size), size)
+    empty = pltpu.make_async_copy(blank, out_ref.at[mine], sem.at[5])
+    empty.start()
     half[pl.ds(7, tiles, stride=8), :] = jnp.zeros((tiles, LANES), F32)
     for copy in copies[:3]:
         copy.wait()
@@ -258,24 +262,27 @@
     parts = [value] + [pltpu.roll(value, LANES - tiles * s, axis=1) for s in range(1, 4)]
     turned = turn(jnp.concatenate(parts, axis=0))
     half[pl.ds(6, tiles, stride=8), :] = turned[:tiles]
-    out_ref[pl.ds(pl.multiple_of((1 - panel) * size, size), size), :] = half[...]
+    full = pltpu.make_async_copy(half, out_ref.at[other], sem.at[6])
+    full.start()
+    empty.wait()
+    full.wait()
 
 
 def gather_call(values, base, fractions, near, far, tiles):
-    vmem = pl.BlockSpec(memory_space=pltpu.VMEM)
     anywhere = pl.BlockSpec(memory_space=pl.ANY)
     return pl.pallas_call(
         gather_kernel,
         out_shape=jax.ShapeDtypeStruct((16 * tiles, LANES), F32),
         in_specs=[anywhere] * 5,
-        out_specs=vmem,
+        out_specs=anywhere,
         scratch_shapes=[
             pltpu.VMEM(values.shape, F32),
             pltpu.VMEM(base.shape, base.dtype),
             pltpu.VMEM(fractions.shape, F32),
             pltpu.VMEM((2, *near.shape), F32),
             pltpu.VMEM((8 * tiles, LANES), F32),
-            pltpu.SemaphoreType.DMA((5,)),
+            pltpu.VMEM((8 * tiles, LANES), F32),
+            pltpu.SemaphoreType.DMA((7,)),
         ],
         compiler_params=pltpu.CompilerParams(vmem_limit_bytes=GATHER_VMEM),
         cost_estimate=pl.CostEstimate(flops=10**6, bytes_accessed=2**18, transcendentals=0),

time: 55.1 us -> 55 us (level)
  no operation moved by 1% of the time
where the time goes in v6:
time: 55 us; the launch traced here: 54.7 us
  Pallas kernels  24.7 us (45%)
  starting transfers between devices  17.9 us (33%)
  waiting for transfers between devices  11.9 us (22%)
    pallas_call x2, Pallas kernels, section_call(): pl.pallas_call(functools.partial(section_kernel, tiles_here, merge, cols,...  15.9 us
    all_to_all x1, starting transfers between devices, on_device(): lax.all_to_all(sent, ('panel', 'tile'), split_axis=0, concat_axis=0, tile...  12.4 us
    all_to_all x1, waiting for transfers between devices, on_device(): lax.all_to_all(sent, ('panel', 'tile'), split_axis=0, concat_axis=0, tile...  6.75 us
    ppermute x4, starting transfers between devices, exchanged(): return lax.ppermute(x, axis, pairs + [(j, i) for i, j in pairs])  5.56 us
    ppermute x4, waiting for transfers between devices, exchanged(): return lax.ppermute(x, axis, pairs + [(j, i) for i, j in pairs])  5.18 us
    pallas_call x1, Pallas kernels, payload_call(): pl.pallas_call(payload_kernel, out_shape=points, in_specs=[anywhere] * 3,...  3.68 us
    pallas_call x1, Pallas kernels, columns_call(): pl.pallas_call(columns_kernel, out_shape=(edge, edge), in_specs=[anywhere...  2.06 us
    pallas_call x1, Pallas kernels, gather_call(): pl.pallas_call(gather_kernel, out_shape=jax.ShapeDtypeStruct((16 * tiles,...  1.64 us
  transfers between devices with their start and end apart: 5, of which 3 were waited for; matrix products, arithmetic and copies ran while one was open for 0% of the time, Pallas kernels for 26%

profile of v6, /device:TPU:4, one launch (start us, length us, event | category | flops | bytes accessed | tf_op | source)
XLA Modules:
  0.0 54.7 jit_solution(17589846337815889703)
XLA Ops:
  0.0 0.0 copy-start
  0.0 0.0 copy-start.1
  0.0 1.4 %faces.1 = (f32[32,32,128]{2,1,0:T(8,128)S(1)}, f32[32,32,128]{2,1,0:T(8,128)S(1)}) custom-call(f32[8,8,32,512]{3,2,1,0:T(8,128)} %bitcast.19), custom_call_target="tpu_custom_call" | custom-call | flops 1000000 | bytes 2097152 | tf_op jit(solution)/shard_map/faces/pallas_call | solution.py:98
  1.4 1.3 %collective-permute-start.2 = (f32[32,32,128]{2,1,0:T(8,128)S(1)}, f32[32,32,128]{2,1,0:T(8,128)S(1)}, u32[]{:S(2)}, u32[]{:S(2)}) collective-permute-start(f32[32,32,128]{2,1,0:T(8,128)S(1)} %get-tuple-element.11), channel_id=1, source_target_pairs={{0,1},{2,3},{1,0},{3,2},{4,5},{6,7},{5,4},{7,6},{8,9},{10,11},{9,8... | collective-permute-start | bytes 1572872 | tf_op jit(solution)/shard_map/ppermute | solution.py:608
  2.7 3.5 %collective-permute-start.3 = (f32[32,32,128]{2,1,0:T(8,128)S(1)}, f32[32,32,128]{2,1,0:T(8,128)S(1)}, u32[]{:S(2)}, u32[]{:S(2)}) collective-permute-start(f32[32,32,128]{2,1,0:T(8,128)S(1)} %get-tuple-element.12), channel_id=1, source_target_pairs={{1,2},{2,1},{5,6},{6,5},{9,10},{10,9},{13,14},{14,13},{17,18},{18,... | collective-permute-start | bytes 1572872 | tf_op jit(solution)/shard_map/ppermute | solution.py:608
  6.2 0.0 copy-start.3
  6.2 2.1 %columns.1 = (f32[2,9,8,512]{3,2,1,0:T(8,128)}, f32[2,9,8,512]{3,2,1,0:T(8,128)}) custom-call(f32[8,8,32,512]{3,2,1,0:T(8,128)} %bitcast.20, s32[4,32]{1,0:T(4,128)} %bitcast.17), custom_call_target="tpu_custom_call" | custom-call | flops 1000000 | bytes 1048576 | tf_op jit(solution)/shard_map/columns/pallas_call | solution.py:147
  8.3 0.1 collective-permute-start
  8.4 0.7 %collective-permute-start.1 = (f32[2,9,8,512]{3,2,1,0:T(8,128)}, f32[2,9,8,512]{3,2,1,0:T(8,128)S(1)}, u32[]{:S(2)}, u32[]{:S(2)}) collective-permute-start(f32[2,9,8,512]{3,2,1,0:T(8,128)} %get-tuple-element.10), channel_id=1, source_target_pairs={{4,8},{12,16},{20,24},{28,32},{36,40},{44,48},{52,56},{60,64},{68,... | collective-permute-start | bytes 884744 | tf_op jit(solution)/shard_map/ppermute | solution.py:608
  9.1 0.0 copy-done
  9.1 0.0 copy-done.1
  9.1 3.7 %payload.1.values_ref = f32[64,128]{1,0:T(8,128)S(1)} custom-call(f32[8,8,32,512]{3,2,1,0:T(8,128)} %bitcast.21, s32[4,32]{1,0:T(4,128)S(1)} %bitcast.15, f32[2,4,32]{2,1,0:T(4,128)S(1)} %bitcast.13), custom_call_target="tpu_custom_call" | custom-call | flops 1000000000 | bytes 6291456 | tf_op jit(solution)/shard_map/payload/pallas_call | solution.py:199
  12.8 2.4 %collective-permute-done.2.near_ref.refs_4_ = f32[32,32,128]{2,1,0:T(8,128)S(1)} collective-permute-done((f32[32,32,128]{2,1,0:T(8,128)S(1)}, f32[32,32,128]{2,1,0:T(8,128)S(1)}, u32[]{:S(2)}, u32[]{:S(2)}) %collective-permute-start.2) | collective-permute-done | bytes 524320 | tf_op jit(solution)/shard_map/ppermute | solution.py:608
  15.2 2.8 %collective-permute-done.3.far_ref.refs_5_ = f32[32,32,128]{2,1,0:T(8,128)S(1)} collective-permute-done((f32[32,32,128]{2,1,0:T(8,128)S(1)}, f32[32,32,128]{2,1,0:T(8,128)S(1)}, u32[]{:S(2)}, u32[]{:S(2)}) %collective-permute-start.3) | collective-permute-done | bytes 524320 | tf_op jit(solution)/shard_map/ppermute | solution.py:608
  18.0 1.6 %gather.1 = f32[512,128]{1,0:T(8,128)} custom-call(f32[64,128]{1,0:T(8,128)S(1)} %payload.1.values_ref, s32[4,32]{1,0:T(4,128)S(1)} %bitcast.16, f32[2,4,32]{2,1,0:T(4,128)S(1)} %bitcast.14, f32[32,32,128]{2,1,0:T(8,128)S(1)} %collective-permute-done.2.near_ref.refs_4_, f32[32,32,128]{2,1,0:T(8,128)S(1)} %collective-permute-done.3.far_ref.refs_5_), custom_call_target="tpu_custom_call" | custom-call | flops 1000000 | bytes 262144 | tf_op jit(solution)/shard_map/gather/pallas_call | solution.py:273
  19.6 12.4 %all-to-all-start = ((f32[64,8,128]{2,1,0:T(8,128)}), f32[64,8,128]{2,1,0:T(8,128)}, u32[]{:S(2)}, u32[]{:S(2)}) async-start(f32[64,8,128]{2,1,0:T(8,128)} %bitcast.7), calls=%async_computation | async-start | bytes 524288 | tf_op jit(solution)/shard_map/all_to_all | solution.py:635
  32.0 0.0 collective-permute-done.refs_2_
  32.0 0.0 collective-permute-done.1.refs_3_
  32.0 0.0 copy-done.3
  32.0 0.0 copy-start.2
  32.0 7.1 %inner.1.refs_8_ = f32[8,8,32,512]{3,2,1,0:T(8,128)} custom-call(f32[4,16,128]{2,1,0:T(8,128)S(1)} %copy-done.3, f32[8,8,32,512]{3,2,1,0:T(8,128)} %bitcast.22, f32[2,9,8,512]{3,2,1,0:T(8,128)S(1)} %collective-permute-done.refs_2_, f32[2,9,8,512]{3,2,1,0:T(8,128)S(1)} %collective-permute-done.1.refs_3_, ...), custom_call_target="tpu_custom_call" | custom-call | flops 19999999655936 | bytes 8388608 | tf_op jit(solution)/shard_map/inner/pallas_call | solution.py:591
  39.1 6.8 %all-to-all-done = f32[64,8,128]{2,1,0:T(8,128)} async-done(((f32[64,8,128]{2,1,0:T(8,128)}), f32[64,8,128]{2,1,0:T(8,128)}, u32[]{:S(2)}, u32[]{:S(2)}) %all-to-all-start) | async-done | bytes 262176 | tf_op jit(solution)/shard_map/all_to_all | solution.py:635
  45.9 0.0 copy-done.2
  45.9 8.8 %outer.1 = f32[8,8,32,512]{3,2,1,0:T(8,128)} custom-call(f32[4,16,128]{2,1,0:T(8,128)S(1)} %copy-done.3, f32[8,8,32,512]{3,2,1,0:T(8,128)} %bitcast.23, f32[2,9,8,512]{3,2,1,0:T(8,128)S(1)} %collective-permute-done.refs_2_, f32[2,9,8,512]{3,2,1,0:T(8,128)S(1)} %collective-permute-done.1.refs_3_, ...), custom_call_target="tpu_custom_call", output_to_operand_aliasing={{}: (8, {})} | custom-call | flops 19999999655936 | bytes 8388608 | tf_op jit(solution)/shard_map/outer/pallas_call | solution.py:591
Async XLA Ops:
  0.0 9.1 %copy-start = (f32[1,1,2,32,4]{3,4,2,1,0:T(4,128)S(1)}, f32[1,1,2,32,4]{3,4,2,1,0:T(4,128)}, u32[]{:S(2)}) copy-start(f32[1,1,2,32,4]{3,4,2,1,0:T(4,128)} %param.7) | copy-start | bytes 3076
  0.0 9.1 %copy-start.1 = (s32[1,1,32,4]{2,3,1,0:T(4,128)S(1)}, s32[1,1,32,4]{2,3,1,0:T(4,128)}, u32[]{:S(2)}) copy-start(s32[1,1,32,4]{2,3,1,0:T(4,128)} %param.6) | copy-start | bytes 1540
  1.4 13.8 %collective-permute-start.2 = (f32[32,32,128]{2,1,0:T(8,128)S(1)}, f32[32,32,128]{2,1,0:T(8,128)S(1)}, u32[]{:S(2)}, u32[]{:S(2)}) collective-permute-start(f32[32,32,128]{2,1,0:T(8,128)S(1)} %get-tuple-element.11), channel_id=1, source_target_pairs={{0,1},{2,3},{1,0},{3,2},{4,5},{6,7},{5,4},{7,6},{8,9},{10,11},{9,8... | collective-permute-start | bytes 1572872 | tf_op jit(solution)/shard_map/ppermute | solution.py:608
  2.7 15.3 %collective-permute-start.3 = (f32[32,32,128]{2,1,0:T(8,128)S(1)}, f32[32,32,128]{2,1,0:T(8,128)S(1)}, u32[]{:S(2)}, u32[]{:S(2)}) collective-permute-start(f32[32,32,128]{2,1,0:T(8,128)S(1)} %get-tuple-element.12), channel_id=1, source_target_pairs={{1,2},{2,1},{5,6},{6,5},{9,10},{10,9},{13,14},{14,13},{17,18},{18,... | collective-permute-start | bytes 1572872 | tf_op jit(solution)/shard_map/ppermute | solution.py:608
  6.2 25.8 %copy-start.3 = (f32[4,16,128]{2,1,0:T(8,128)S(1)}, f32[4,16,128]{2,1,0:T(8,128)}, u32[]{:S(2)}) copy-start(f32[4,16,128]{2,1,0:T(8,128)} %constant.2.clone.refs_0_) | copy-start | bytes 98308
  8.3 23.7 %collective-permute-start = (f32[2,9,8,512]{3,2,1,0:T(8,128)}, f32[2,9,8,512]{3,2,1,0:T(8,128)S(1)}, u32[]{:S(2)}, u32[]{:S(2)}) collective-permute-start(f32[2,9,8,512]{3,2,1,0:T(8,128)} %get-tuple-element.9), channel_id=1, source_target_pairs={{0,4},{8,12},{16,20},{24,28},{32,36},{40,44},{48,52},{56,60},{64,6... | collective-permute-start | bytes 884744 | tf_op jit(solution)/shard_map/ppermute | solution.py:608
  8.4 23.6 %collective-permute-start.1 = (f32[2,9,8,512]{3,2,1,0:T(8,128)}, f32[2,9,8,512]{3,2,1,0:T(8,128)S(1)}, u32[]{:S(2)}, u32[]{:S(2)}) collective-permute-start(f32[2,9,8,512]{3,2,1,0:T(8,128)} %get-tuple-element.10), channel_id=1, source_target_pairs={{4,8},{12,16},{20,24},{28,32},{36,40},{44,48},{52,56},{60,64},{68,... | collective-permute-start | bytes 884744 | tf_op jit(solution)/shard_map/ppermute | solution.py:608
  19.6 26.3 %all-to-all-start = ((f32[64,8,128]{2,1,0:T(8,128)}), f32[64,8,128]{2,1,0:T(8,128)}, u32[]{:S(2)}, u32[]{:S(2)}) async-start(f32[64,8,128]{2,1,0:T(8,128)} %bitcast.7), calls=%async_computation | async-start | bytes 524288 | tf_op jit(solution)/shard_map/all_to_all | solution.py:635
  32.0 13.9 %copy-start.2 = (s32[1,1,32,4]{2,3,1,0:T(4,128)S(1)}, s32[1,1,32,4]{2,3,1,0:T(4,128)}, u32[]{:S(2)}) copy-start(s32[1,1,32,4]{2,3,1,0:T(4,128)} %param.8) | copy-start | bytes 1540
